TPU v7x, 32 devices: a whole 2x2x4 slice. The times are simulated.
32 devices in a mesh: seq: 8 (over z, x), exp: 4 (over y, core).
Axes of the slice: x: 2, y: 2, z: 4, core: 2. Of those that a mesh axis runs over, the one named last changes fastest.
Arguments:
- x_in: bfloat16 [512, 8192], P('seq', 'exp'), may hold values from -6 to 6
- z_in: bfloat16 [512, 8192], P('seq', 'exp'), may hold values from -6 to 6
- conv_weight: float32 [4, 8192], P(None, 'exp'), may hold values from -3 to 3
- conv_bias: float32 [8192], P('exp'), may hold values from -3 to 3
- x_proj: bfloat16 [8192, 544], P('exp'), may hold values from -0.0625 to 0.0625
- dt_proj: bfloat16 [512, 8192], P(None, 'exp'), may hold values from -0.25 to 0.25
- dt_bias: float32 [8192], P('exp'), may hold values from -7 to -2.3
- a_log: float32 [8192, 16], P('exp'), may hold values from -6 to 0
- d_skip: float32 [8192], P('exp'), may hold values from 0.5 to 1.5
- out_proj: bfloat16 [8192, 4096], P('exp', 'seq'), may hold values from -0.0625 to 0.0625
- resid: bfloat16 [512, 4096], P('seq', 'exp'), may hold values from -8 to 8
- norm_gain: float32 [4096], replicated, may hold values from 0.5 to 1.5
- routes: int32 [512, 2], P('seq'), may hold values from 0 to 3, all different within a row; in each aligned block of 64 rows (0 to 63, 64 to 127, ...) at most 34 rows name the same one
- route_gate: float32 [512, 2], P('seq'), may hold values from 0.1 to 0.9
- w_gate: bfloat16 [4, 4096, 12288], P('exp', None, 'seq'), may hold values from -0.09375 to 0.09375
- w_up: bfloat16 [4, 4096, 12288], P('exp', None, 'seq'), may hold values from -0.09375 to 0.09375
- w_down: bfloat16 [4, 12288, 4096], P('exp', 'seq'), may hold values from -0.078125 to 0.078125
Outputs:
- layer_out: bfloat16 [512, 4096], P('seq', 'exp')
Inputs may be any that keep to these rules, and one draw needn't show every extreme that they name: `routes`: the 2 experts of a position differ; among the 64 positions of one index of seq no expert is named more than 34 times, and in some such block one expert is named exactly 34 times.
All inputs are finite; a program needn't handle non-finite values.
Results may differ from a plain program's by a relative error of at most 0.008.
Values may be sent and summed in bfloat16 or wider, within the bound.
No kernel may reach another device: no remote copies, remote signals or barrier semaphores. Data moves between devices by JAX's collectives and lax.ppermute only.
A program may use at most 128 MiB of HBM per device.

v0:
```python
import functools
import math

import jax
import jax.numpy as jnp
from jax import lax
from jax.experimental import pallas as pl
from jax.experimental.pallas import tpu as pltpu
from jax.sharding import PartitionSpec as P

eps = 1e-05
LOG2E = 1.4426950408889634
MIB = 1 << 20


def tile_of(size, most=512):
    return max(t for t in range(128, most + 1, 128) if size % t == 0)


def after(value, *others):
    return lax.optimization_barrier((value, *others))[0]


def whole_vmem():
    return pl.BlockSpec(memory_space=pltpu.VMEM)


def lanes_of(width):
    return pl.ds(pl.multiple_of(pl.program_id(0) * width, width), width)


def whole_smem():
    return pl.BlockSpec(memory_space=pltpu.SMEM)


def conv_kernel(x_ref, halo_ref, weight_ref, bias_ref, proj_ref, xconv_ref, partial_ref):
    rows = x_ref.shape[0]
    taps = weight_ref.shape[0]
    across = lanes_of(x_ref.shape[1])
    extended = jnp.concatenate(
        [halo_ref[:, across].astype(jnp.float32), x_ref[...].astype(jnp.float32)], axis=0
    )
    pad = halo_ref.shape[0]
    conv = jnp.zeros(x_ref.shape, jnp.float32) + bias_ref[...]
    for tap in range(taps):
        start = pad - (taps - 1) + tap
        conv = conv + weight_ref[tap : tap + 1, :] * extended[start : start + rows]
    xconv = (conv / (1.0 + jnp.exp(-conv))).astype(jnp.bfloat16)
    xconv_ref[...] = xconv

    @pl.when(pl.program_id(0) == 0)
    def _():
        partial_ref[...] = jnp.zeros_like(partial_ref)

    partial_ref[...] += lax.dot_general(
        xconv, proj_ref[...], (((1,), (1,)), ((), ())), preferred_element_type=jnp.float32
    )


def conv_and_project(x_in, halo, conv_weight, conv_bias, x_proj_t):
    rows, channels = x_in.shape
    width = tile_of(channels, 1024)
    columns = x_proj_t.shape[0]
    return pl.pallas_call(
        conv_kernel,
        grid=(channels // width,),
        in_specs=[
            pl.BlockSpec((rows, width), lambda i: (0, i)),
            whole_vmem(),
            pl.BlockSpec((conv_weight.shape[0], width), lambda i: (0, i)),
            pl.BlockSpec((1, width), lambda i: (0, i)),
            pl.BlockSpec((columns, width), lambda i: (0, i)),
        ],
        out_specs=[
            pl.BlockSpec((rows, width), lambda i: (0, i)),
            pl.BlockSpec((rows, columns), lambda i: (0, 0)),
        ],
        out_shape=[
            jax.ShapeDtypeStruct((rows, channels), jnp.bfloat16),
            jax.ShapeDtypeStruct((rows, columns), jnp.float32),
        ],
        name="conv_project",
    )(x_in, halo, conv_weight, conv_bias, x_proj_t)


def softplus(v):
    return jnp.maximum(v, 0.0) + jnp.log1p(jnp.exp(-jnp.abs(v)))


def ends_kernel(count, *refs):
    parts = refs[:count]
    proj_ref, bias_ref, rate_ref, x_ref, info_ref = refs[count : count + 5]
    size_ref, load_ref, b_ref, c_ref, low_ref, drive_ref = refs[count + 5 :]
    rows, width = x_ref.shape
    states = rate_ref.shape[0]
    low_rank = low_ref.shape[1]
    groups = width // 128

    @pl.when(pl.program_id(0) == 0)
    def _():
        total = parts[0][...]
        for part in parts[1:]:
            total = total + part[...]
        low_ref[...] = total[:, :low_rank].astype(jnp.bfloat16)
        b_mat = total[:, low_rank : low_rank + states]
        c_mat = total[:, low_rank + states : low_rank + 2 * states]
        b_ref[...] = jnp.broadcast_to(b_mat[:, :, None], b_ref.shape)
        c_ref[...] = jnp.broadcast_to(c_mat[:, :, None], c_ref.shape)

    size = softplus(
        jnp.dot(low_ref[...], proj_ref[...], preferred_element_type=jnp.float32) + bias_ref[...]
    )
    size_ref[...] = size
    drive_ref[...] = size * x_ref[...].astype(jnp.float32)
    rates = rate_ref[...]

    def step(block, state):
        start = pl.multiple_of(block * 8, 8)
        sizes = size_ref[pl.ds(start, 8), :]
        drives = drive_ref[pl.ds(start, 8), :]
        state = list(state)
        for i in range(8):
            b_now = b_ref[start + i]
            for g in range(groups):
                lanes = slice(g * 128, g * 128 + 128)
                decay = jnp.exp2(sizes[i : i + 1, lanes] * rates[:, lanes])
                state[g] = decay * state[g] + drives[i : i + 1, lanes] * b_now
        return tuple(state)

    zero = jnp.zeros((states, 128), jnp.float32)
    state = lax.fori_loop(0, rows // 8, step, (zero,) * groups)
    total = jnp.sum(size, axis=0, keepdims=True)
    high = total.astype(jnp.bfloat16).astype(jnp.float32)
    low = total - high
    rest = info_ref[: load_ref.shape[0] - states - 2, :]
    load_ref[...] = jnp.concatenate(
        [jnp.concatenate(state, axis=1), high, low, rest], axis=0
    ).astype(jnp.bfloat16)


def scan_ends(partials, dt_proj, dt_bias, rates, xconv, info):
    rows, channels = xconv.shape
    states = rates.shape[0]
    width = tile_of(channels, 1024)
    load_rows = -(-(states + 2) // 8) * 8
    wide = jax.ShapeDtypeStruct((rows, states, 128), jnp.float32)
    return pl.pallas_call(
        functools.partial(ends_kernel, len(partials)),
        grid=(channels // width,),
        in_specs=[
            *[whole_vmem() for _ in partials],
            pl.BlockSpec((dt_proj.shape[0], width), lambda i: (0, i)),
            pl.BlockSpec((1, width), lambda i: (0, i)),
            pl.BlockSpec((states, width), lambda i: (0, i)),
            pl.BlockSpec((rows, width), lambda i: (0, i)),
            pl.BlockSpec((info.shape[0], width), lambda i: (0, i)),
        ],
        out_specs=[
            pl.BlockSpec((rows, width), lambda i: (0, i)),
            pl.BlockSpec((load_rows, width), lambda i: (0, i)),
            pl.BlockSpec(wide.shape, lambda i: (0, 0, 0)),
            pl.BlockSpec(wide.shape, lambda i: (0, 0, 0)),
        ],
        out_shape=[
            jax.ShapeDtypeStruct((rows, channels), jnp.float32),
            jax.ShapeDtypeStruct((load_rows, channels), jnp.bfloat16),
            wide,
            wide,
        ],
        scratch_shapes=[
            pltpu.VMEM((rows, dt_proj.shape[0]), jnp.bfloat16),
            pltpu.VMEM((rows, width), jnp.float32),
        ],
        name="scan_ends",
    )(*partials, dt_proj, dt_bias, rates, xconv, info)


def mix_kernel(z_count, x_count, z_place, x_place, *refs):
    count = z_count * x_count
    loads = refs[:count]
    size_ref, x_ref, z_ref, b_ref, c_ref, rate_ref, skip_ref, out_ref = refs[count : count + 8]
    drive_ref, y_ref, load_ref = refs[count + 8 :]
    across = lanes_of(x_ref.shape[1])
    for k in range(count):
        z_from = lax.rem(z_place[0] + k // x_count, z_count)
        x_from = lax.rem(x_place[0] + k % x_count, x_count)
        load_ref[z_from * x_count + x_from] = loads[k][:, across].astype(jnp.float32)
    rows, width = x_ref.shape
    states = rate_ref.shape[0]
    groups = width // 128
    rates = rate_ref[...]
    x_f = x_ref[...].astype(jnp.float32)
    drive_ref[...] = size_ref[...] * x_f

    def earlier(j, state):
        block = load_ref[j]
        total = block[states : states + 1] + block[states + 1 : states + 2]
        return jnp.exp2(total * rates) * state + block[:states]

    place = z_place[0] * x_count + x_place[0]
    incoming = lax.fori_loop(0, place, earlier, jnp.zeros((states, width), jnp.float32))

    def step(block, state):
        start = pl.multiple_of(block * 8, 8)
        sizes = size_ref[pl.ds(start, 8), :]
        drives = drive_ref[pl.ds(start, 8), :]
        state = list(state)
        outs = [[None] * 8 for _ in range(groups)]
        for i in range(8):
            b_now = b_ref[start + i]
            c_now = c_ref[start + i]
            for g in range(groups):
                lanes = slice(g * 128, g * 128 + 128)
                decay = jnp.exp2(sizes[i : i + 1, lanes] * rates[:, lanes])
                state[g] = decay * state[g] + drives[i : i + 1, lanes] * b_now
                outs[g][i] = jnp.sum(state[g] * c_now, axis=0, keepdims=True)
        for g in range(groups):
            y_ref[pl.ds(start, 8), g * 128 : g * 128 + 128] = jnp.concatenate(outs[g], axis=0)
        return tuple(state)

    start_state = tuple(incoming[:, g * 128 : g * 128 + 128] for g in range(groups))
    lax.fori_loop(0, rows // 8, step, start_state)
    z_f = z_ref[...].astype(jnp.float32)
    scanned = y_ref[...] + skip_ref[...] * x_f
    out_ref[...] = (scanned * (z_f / (1.0 + jnp.exp(-z_f)))).astype(jnp.bfloat16)


def scan_mix(z_at, x_at, loads, step_size, xconv, z_in, b_wide, c_wide, rates, d_skip):
    rows, channels = xconv.shape
    states = rates.shape[0]
    width = tile_of(channels, 1024)
    flat = [load for pair in loads for load in pair]

    def by_lane(depth):
        return pl.BlockSpec((depth, width), lambda i: (0, i))

    return pl.pallas_call(
        functools.partial(mix_kernel, len(loads), len(loads[0])),
        grid=(channels // width,),
        in_specs=[
            whole_smem(),
            whole_smem(),
            *[whole_vmem() for _ in flat],
            by_lane(rows),
            by_lane(rows),
            by_lane(rows),
            pl.BlockSpec(b_wide.shape, lambda i: (0, 0, 0)),
            pl.BlockSpec(c_wide.shape, lambda i: (0, 0, 0)),
            by_lane(states),
            by_lane(1),
        ],
        out_specs=by_lane(rows),
        out_shape=jax.ShapeDtypeStruct((rows, channels), jnp.bfloat16),
        scratch_shapes=[pltpu.VMEM((rows, width), jnp.float32)] * 2
        + [pltpu.VMEM((len(flat), flat[0].shape[0], width), jnp.float32)],
        name="scan_mix",
    )(z_at, x_at, *flat, step_size, xconv, z_in, b_wide, c_wide, rates, d_skip)


def out_kernel(z_count, counts, z_ref, x_ref, e_ref, keep_pick_ref, send_pick_ref, resid_ref, *refs):
    x_count = len(counts)
    blocks = refs[:z_count]
    keep_ref, send_ref, held_ref, sum_ref = refs[z_count + sum(counts) :]
    weights = list(refs[z_count : z_count + sum(counts)])
    rows = blocks[0].shape[0]
    columns = weights[0].shape[1]
    for r in range(z_count):
        at = pl.multiple_of(lax.rem(z_ref[0] + r, z_count) * rows, rows)
        held_ref[pl.ds(at, rows), :] = blocks[r][...]
    own = pl.ds(pl.multiple_of(e_ref[0] * rows, rows), rows)
    for i, count in enumerate(counts):
        at = pl.ds(pl.multiple_of(lax.rem(x_ref[0] + i, x_count) * columns, columns), columns)
        start, parts = 0, []
        for _ in range(count):
            weight = weights.pop(0)
            depth = weight.shape[0]
            parts.append(
                jnp.dot(
                    held_ref[:, start : start + depth],
                    weight[...],
                    preferred_element_type=jnp.float32,
                )
            )
            start += depth
        sum_ref[...] = functools.reduce(jnp.add, parts)
        sum_ref[own, :] += resid_ref[:, at].astype(jnp.float32)
        summed = sum_ref[...].astype(jnp.bfloat16)
        for pick_ref, out_ref in ((keep_pick_ref, keep_ref), (send_pick_ref, send_ref)):
            out_ref[:, at] = jnp.dot(
                pick_ref[...], summed, preferred_element_type=jnp.float32
            ).astype(jnp.bfloat16)


def out_product(z_at, x_at, e_at, keep_pick, send_pick, resid, blocks, weights):
    rows, depth = blocks[0].shape
    z_count, x_count = len(blocks), len(weights)
    counts = [len(parts) for parts in weights]
    columns = weights[0][0].shape[1]
    return pl.pallas_call(
        functools.partial(out_kernel, z_count, counts),
        in_specs=[whole_smem()] * 3 + [whole_vmem()] * (3 + z_count + sum(counts)),
        out_specs=[whole_vmem()] * 2,
        out_shape=[jax.ShapeDtypeStruct((keep_pick.shape[0], x_count * columns), jnp.bfloat16)] * 2,
        scratch_shapes=[
            pltpu.VMEM((z_count * rows, depth), jnp.bfloat16),
            pltpu.VMEM((z_count * rows, columns), jnp.float32),
        ],
        compiler_params=pltpu.CompilerParams(vmem_limit_bytes=16 * MIB),
        name="out_product",
    )(
        z_at,
        x_at,
        e_at,
        keep_pick,
        send_pick,
        resid,
        *blocks,
        *[part for parts in weights for part in parts],
    )


def hidden_kernel(z_count, x_count, z_ref, x_ref, *refs):
    count = z_count * x_count
    chunks = refs[:count]
    gain_ref, gate_ref, up_ref, act_ref, scaled_ref = refs[count:]
    rows, depth = chunks[0].shape
    padded = scaled_ref.shape[0] // x_count

    def filled(chunk):
        h = chunk[...].astype(jnp.float32)
        if padded == rows:
            return h
        return jnp.concatenate([h, jnp.zeros((padded - rows, depth), jnp.float32)], axis=0)

    @pl.when(pl.program_id(0) == 0)
    def _():
        for i in range(x_count):
            own = [chunks[r * x_count + i] for r in range(z_count)]
            squares = jnp.zeros((padded, 1), jnp.float32)
            for chunk in own:
                h = filled(chunk)
                squares = squares + jnp.sum(h * h, axis=1, keepdims=True)
            scale = lax.rsqrt(squares / (depth * z_count) + eps)
            down = pl.multiple_of(lax.rem(x_ref[0] + i, x_count) * padded, padded)
            for r, chunk in enumerate(own):
                z_at = lax.rem(z_ref[0] + r, z_count)
                across = pl.multiple_of(z_at * depth, depth)
                h = filled(chunk)
                scaled_ref[pl.ds(down, padded), pl.ds(across, depth)] = (
                    h * scale * gain_ref[z_at]
                ).astype(jnp.bfloat16)

    scaled = scaled_ref[...]
    gate = jnp.dot(scaled, gate_ref[0], preferred_element_type=jnp.float32)
    upper = jnp.dot(scaled, up_ref[0], preferred_element_type=jnp.float32)
    act_ref[...] = (gate / (1.0 + jnp.exp(-gate)) * upper).astype(jnp.bfloat16)


def expert_hidden(z_at, x_at, chunks, gain, w_gate, w_up):
    z_count, x_count = len(chunks), len(chunks[0])
    rows, depth = chunks[0][0].shape
    columns = w_gate.shape[2]
    width = tile_of(columns, 256)
    padded = -(-rows // 16) * 16 * x_count
    gain = gain.reshape(z_count, 1, depth)
    weight_spec = pl.BlockSpec((1, depth * z_count, width), lambda n: (0, 0, n))
    return pl.pallas_call(
        functools.partial(hidden_kernel, z_count, x_count),
        grid=(columns // width,),
        in_specs=[whole_smem()] * 2
        + [whole_vmem()] * (z_count * x_count + 1)
        + [weight_spec, weight_spec],
        out_specs=pl.BlockSpec((padded, width), lambda n: (0, n)),
        out_shape=jax.ShapeDtypeStruct((padded, columns), jnp.bfloat16),
        scratch_shapes=[pltpu.VMEM((padded, depth * z_count), jnp.bfloat16)],
        compiler_params=pltpu.CompilerParams(vmem_limit_bytes=50 * MIB),
        name="expert_hidden",
    )(z_at, x_at, *[chunk for pair in chunks for chunk in pair], gain, w_gate, w_up)


def down_kernel(x_count, x_ref, blocks_ref, act_ref, weight_ref, *refs):
    outs, held_ref = refs[:-1], refs[-1]
    held_ref[...] = jnp.dot(act_ref[...], weight_ref[0], preferred_element_type=jnp.float32)
    rows = outs[0].shape[0]
    padded = held_ref.shape[0] // x_count
    for k in range(len(outs) // x_count):

        @pl.when(pl.program_id(0) == k)
        def _(k=k):
            for i in range(x_count):
                start = pl.multiple_of(lax.rem(x_ref[0] + i, x_count) * padded, padded)
                outs[k * x_count + i][...] = held_ref[pl.ds(start, rows), :].astype(jnp.bfloat16)


def expert_down(x_at, blocks, x_count, z_count, rows, act, w_down):
    padded, depth = act.shape
    columns = w_down.shape[2] // z_count
    width = tile_of(columns)
    tiles = columns // width
    count = blocks.shape[0]

    def out_spec(k):
        def place(m, n, x, blocks):
            return (0, jnp.where(m == k, n, jnp.where(m < k, 0, tiles - 1)))

        return pl.BlockSpec((rows, width), place)

    outs = pl.pallas_call(
        functools.partial(down_kernel, x_count),
        grid_spec=pltpu.PrefetchScalarGridSpec(
            num_scalar_prefetch=2,
            grid=(count, tiles),
            in_specs=[
                pl.BlockSpec((padded, depth), lambda m, n, x, blocks: (0, 0)),
                pl.BlockSpec(
                    (1, depth, width), lambda m, n, x, blocks: (0, 0, blocks[m] * tiles + n)
                ),
            ],
            out_specs=[out_spec(k) for k in range(count) for _ in range(x_count)],
            scratch_shapes=[pltpu.VMEM((padded, width), jnp.float32)],
        ),
        out_shape=[jax.ShapeDtypeStruct((rows, columns), jnp.bfloat16)] * (count * x_count),
        compiler_params=pltpu.CompilerParams(vmem_limit_bytes=50 * MIB),
        name="expert_down",
    )(x_at, blocks, act, w_down)
    return [outs[k * x_count : (k + 1) * x_count] for k in range(count)]


def per_device(
    x_in,
    z_in,
    conv_weight,
    conv_bias,
    x_proj,
    dt_proj,
    dt_bias,
    a_log,
    d_skip,
    out_proj,
    resid,
    norm_gain,
    routes,
    route_gate,
    w_gate,
    w_up,
    w_down,
):
    row_count, channels = x_in.shape
    seq_count = lax.axis_size("seq")
    exp_count = lax.axis_size("exp")
    x_count = seq_count // exp_count
    z_count = exp_count
    seq_at = lax.axis_index("seq")
    exp_at = lax.axis_index("exp")
    z_at, x_at = seq_at // x_count, seq_at % x_count
    z_one = z_at.reshape(1).astype(jnp.int32)
    x_one = x_at.reshape(1).astype(jnp.int32)
    e_one = exp_at.reshape(1).astype(jnp.int32)
    top_count = routes.shape[1]
    capacity = row_count * top_count * 17 // (16 * exp_count)
    pitch = capacity
    feature_slice = resid.shape[1]

    def from_z(block, r):
        pairs = [
            (((z + r) % z_count) * x_count + x, z * x_count + x)
            for z in range(z_count)
            for x in range(x_count)
        ]
        return lax.ppermute(block, "seq", pairs)

    def from_x(block, i):
        pairs = [
            (z * x_count + (x + i) % x_count, z * x_count + x)
            for z in range(z_count)
            for x in range(x_count)
        ]
        return lax.ppermute(block, "seq", pairs)

    turns = sorted(range(1, z_count), key=lambda r: min(r, z_count - r))

    def gathered(block):
        rows = {(0, 0): block}
        others = range(1, x_count)
        for i in others:
            rows[0, i] = from_x(block, i)
        sent = block
        for k, r in enumerate(turns):
            if k >= 2:
                sent = after(sent, rows[turns[k - 2], 0], *[rows[0, i] for i in others])
            rows[r, 0] = from_z(sent, r)
        for k, r in enumerate(turns):
            earlier = turns[max(k - 2, 0) : max(k - 1, 0)] if r != turns[-1] else turns[:k]
            forward = after(rows[r, 0], *[rows[q, i] for q in earlier for i in others])
            for i in others:
                rows[r, i] = from_x(forward, i)
        return [[rows[r, i] for i in range(x_count)] for r in range(z_count)]

    y_count = exp_count // 2

    def other_core(block):
        return lax.ppermute(block, "exp", [(e ^ 1, e) for e in range(exp_count)])

    def from_y(block, r):
        pairs = [
            ((y + r) % y_count * 2 + core, y * 2 + core)
            for y in range(y_count)
            for core in range(2)
        ]
        return lax.ppermute(block, "exp", pairs)

    swap = [
        ((e * x_count + x) * exp_count + z, (z * x_count + x) * exp_count + e)
        for z in range(z_count)
        for x in range(x_count)
        for e in range(exp_count)
    ]

    halo = lax.ppermute(
        x_in[row_count - 8 :], "seq", [(i, i + 1) for i in range(seq_count - 1)]
    )

    xconv, partial = conv_and_project(x_in, halo, conv_weight, conv_bias[None], x_proj.T)
    resid_here = lax.ppermute(resid, ("seq", "exp"), swap)

    chip_sum = partial + other_core(after(partial, resid_here))
    a_log, routes, route_gate = lax.optimization_barrier(
        (a_log, routes, route_gate, chip_sum)
    )[:3]
    rates = -jnp.exp(a_log.T) * LOG2E

    def part_of(v):
        return v.astype(jnp.bfloat16).astype(jnp.float32)

    gate_high = part_of(route_gate)
    gate_mid = part_of(route_gate - gate_high)
    gate_low = route_gate - gate_high - gate_mid
    info = jnp.stack([routes.astype(jnp.float32), gate_high, gate_mid, gate_low])
    info = info.transpose(0, 2, 1).reshape(4, top_count * row_count)
    info = jnp.pad(info, ((0, 4), (0, channels - top_count * row_count)))

    def slots_of(named):
        flat = named.reshape(-1, row_count * top_count)
        onehot = (flat[:, :, None] == jnp.arange(exp_count, dtype=jnp.int32)).astype(jnp.float32)
        below = jnp.tril(jnp.ones((row_count * top_count,) * 2, jnp.float32), -1)
        counts = jnp.einsum("ij,bje->bie", below, onehot)
        slots = jnp.sum(counts * onehot, axis=2).astype(jnp.int32)
        return slots.reshape(-1, row_count, top_count)

    own_target = (routes - z_at) % exp_count * pitch + slots_of(routes)[0]
    slot_ids = jnp.arange(exp_count * pitch, dtype=jnp.int32)
    choose = jnp.sum(
        (own_target[:, :, None] == slot_ids[None, None, :]).astype(jnp.float32), axis=1
    ).astype(jnp.bfloat16)

    cut = channels * 5 // 16
    uppers = [from_x(after(out_proj, halo)[:cut], i) for i in range(1, x_count)]
    partials = [chip_sum] + [from_y(chip_sum, r) for r in range(1, y_count)]
    step_size, load, b_wide, c_wide = scan_ends(partials, dt_proj, dt_bias[None], rates, xconv, info)
    loads = gathered(after(load, resid_here, *uppers))
    held_proj = after(out_proj, *[part for pair in loads for part in pair])
    lowers = [from_x(held_proj[cut:], i) for i in range(1, x_count)]
    columns = [[out_proj]] + [list(pair) for pair in zip(uppers, lowers)]
    mixed = scan_mix(
        z_one, x_one, loads, step_size, xconv, z_in, b_wide, c_wide, rates, d_skip[None]
    )
    along_z = [mixed] + [from_z(mixed, r) for r in range(1, z_count)]

    first_row = a_log.shape[1] + 2
    spare = after(jnp.stack([loads[r][0][first_row:] for r in range(z_count)]), mixed)
    spare = spare[:, :4, : top_count * row_count].astype(jnp.float32)
    spare = lax.dynamic_slice_in_dim(
        jnp.concatenate([spare, spare]), (z_count - z_at) % z_count, z_count, 0
    ).reshape(z_count, 4, top_count, row_count)
    all_routes = spare[:, 0].transpose(0, 2, 1).astype(jnp.int32)
    all_gates = (spare[:, 1] + spare[:, 2] + spare[:, 3]).transpose(0, 2, 1)
    z_ids = jnp.arange(z_count, dtype=jnp.int32)[:, None, None]
    target = (all_routes * z_count + z_ids) * pitch + slots_of(all_routes)
    target = target.reshape(z_count * row_count, top_count)
    count = z_count * pitch
    exp_late = after(exp_at, mixed)
    y_at, core_at = exp_late // 2, exp_late % 2

    def picked(core):
        experts = (y_at + jnp.arange(y_count, dtype=jnp.int32)) % y_count * 2 + core
        ids = experts[:, None] * count + jnp.arange(count, dtype=jnp.int32)[None, :]
        same = target[None, :, :] == ids.reshape(-1)[:, None, None]
        return jnp.sum(same.astype(jnp.float32), axis=2).astype(jnp.bfloat16)

    here_ids = exp_at * z_count * pitch + jnp.arange(z_count * pitch, dtype=jnp.int32)
    here = target[None, :, :] == here_ids[:, None, None]
    gate_here = jnp.sum(
        jnp.where(here, all_gates.reshape(1, z_count * row_count, top_count), 0.0), axis=(1, 2)
    )[:, None]
    first_here = jnp.sum(here[:, :, 0].astype(jnp.float32), axis=1)[:, None]

    keep, send = out_product(
        z_one, x_one, e_one, picked(core_at), picked(1 - core_at), resid_here, along_z, columns
    )
    over_chip = keep.astype(jnp.float32) + other_core(send).astype(jnp.float32)
    over_chip = over_chip.reshape(y_count, count, feature_slice)
    rows_here = over_chip[0]
    for r in range(1, y_count):
        arrived = from_y(over_chip[r].astype(jnp.bfloat16), y_count - r)
        rows_here = rows_here + arrived.astype(jnp.float32)
    rows_here = rows_here.astype(jnp.bfloat16)

    chunks = gathered(rows_here)
    act = expert_hidden(z_one, x_one, chunks, norm_gain, w_gate, w_up)

    by_distance = sorted(range(1, z_count), key=lambda r: abs(r - z_count // 2)) + [0]
    down, crossed, arrivals = {}, {}, []

    def products(turns_now, rows):
        blocks = jnp.stack([(z_at + r) % z_count for r in turns_now]).astype(jnp.int32)
        outs = expert_down(x_one, blocks, x_count, z_count, exp_count * pitch, rows, w_down)
        down.update(zip(turns_now, outs))

    def over_x(r):
        return functools.reduce(
            jnp.add, [p.astype(jnp.float32) for p in [down[r][0]] + crossed[r]]
        )

    products(by_distance[:1], act)
    products(by_distance[1:-1], act)
    for k, r in enumerate(by_distance):
        if r == 0:
            products([0], after(act, *crossed[by_distance[1]]))
        pieces = down[r][1:]
        if r == 0:
            pieces = [after(piece, arrivals[0]) for piece in pieces]
        elif k >= 2:
            pieces = [after(piece, *crossed[by_distance[k - 2]]) for piece in pieces]
        crossed[r] = [from_x(piece, x_count - i) for i, piece in enumerate(pieces, 1)]
        if r:
            arrivals.append(from_z(over_x(r).astype(jnp.bfloat16), z_count - r))
    total = over_x(0)
    for sent in arrivals:
        total = total + sent.astype(jnp.float32)
    expert_out = total.astype(jnp.bfloat16).astype(jnp.float32)
    expert_out = gate_here * expert_out + first_here * rows_here.astype(jnp.float32)
    expert_out = expert_out.astype(jnp.bfloat16)
    pieces = expert_out.reshape(exp_count, pitch, feature_slice)
    back = []
    for k in range(exp_count):
        piece = lax.dynamic_index_in_dim(pieces, (exp_at - k) % exp_count, 0, keepdims=False)
        pairs = [
            (
                (e * x_count + x) * exp_count + (z + k) % exp_count,
                (z * x_count + x) * exp_count + e,
            )
            for z in range(z_count)
            for x in range(x_count)
            for e in range(exp_count)
        ]
        back.append(lax.ppermute(piece, ("seq", "exp"), pairs))
    back = jnp.concatenate(back, axis=0)
    return jnp.dot(choose, back, preferred_element_type=jnp.float32).astype(jnp.bfloat16)


def solution(mesh):
    return jax.shard_map(
        per_device,
        mesh=mesh,
        in_specs=(
            P("seq", "exp"),
            P("seq", "exp"),
            P(None, "exp"),
            P("exp"),
            P("exp", None),
            P(None, "exp"),
            P("exp"),
            P("exp", None),
            P("exp"),
            P("exp", "seq"),
            P("seq", "exp"),
            P(),
            P("seq", None),
            P("seq", None),
            P("exp", None, "seq"),
            P("exp", None, "seq"),
            P("exp", "seq", None),
        ),
        out_specs=P("seq", "exp"),
        check_vma=False,
    )
```

profile of v0, /device:TPU:5, one launch (start us, length us, event | category | flops | bytes accessed | tf_op | source)
XLA Modules:
  0.0 205.7 jit_solution(6503341661657574008)
XLA Ops:
  0.0 5.9 %collective-permute-start.1 = (bf16[64,1024]{1,0:T(8,128)(2,1)}, bf16[64,1024]{1,0:T(8,128)(2,1)S(1)}, u32[]{:S(2)}, u32[]{:S(2)}) collective-permute-start(bf16[64,1024]{1,0:T(8,128)(2,1)} %param.27), channel_id=1, source_target_pairs={{0,0},{8,1},{16,2},{24,3},{4,4},{12,5},{20,6},{28,7},{1,8},{9,9},{... | collective-permute-start | bytes 393224 | tf_op jit(solution)/shard_map/ppermute | solution.py:524
  6.6 3.1 %collective-permute-start = (bf16[8,2048]{1,0:T(8,128)(2,1)S(1)}, bf16[8,2048]{1,0:T(8,128)(2,1)S(1)}, u32[]{:S(2)}, u32[]{:S(2)}) collective-permute-start(bf16[8,2048]{1,0:T(8,128)(2,1)S(1)} %slice.48), channel_id=1, source_target_pairs={{0,4},{4,8},{8,12},{12,16},{16,20},{20,24},{24,28},{1,5},{5,9},{9,... | collective-permute-start | bytes 98312 | tf_op jit(solution)/shard_map/ppermute | solution.py:519
  11.5 3.6 %conv_project.1 = (bf16[64,2048]{1,0:T(8,128)(2,1)}, f32[64,544]{1,0:T(8,128)}) custom-call(bf16[64,2048]{1,0:T(8,128)(2,1)} %x_ref.1, bf16[8,2048]{1,0:T(8,128)(2,1)} %copy-done.17, f32[4,2048]{1,0:T(4,128)} %weight_ref.4, f32[1,2048]{1,0:T(1,128)} %bitcast.80, bf16[544,2048]{1,0:T(8,128)(2,1)} %bitcast.76), custom_call_target="tpu_custom_call" | custom-call | tf_op jit(solution)/shard_map/conv_project/pallas_call | solution.py:64
  16.8 2.2 %collective-permute-start.4 = (bf16[640,512]{1,0:T(8,128)(2,1)}, bf16[640,512]{1,0:T(8,128)(2,1)S(1)}, u32[]{:S(2)}, u32[]{:S(2)}) collective-permute-start(bf16[640,512]{1,0:T(8,128)(2,1)} %slice.49), channel_id=1, source_target_pairs={{4,0},{0,4},{12,8},{8,12},{20,16},{16,20},{28,24},{24,28},{5,1},{1... | collective-permute-start | bytes 1966088 | tf_op jit(solution)/shard_map/ppermute | solution.py:478
  21.9 2.4 %collective-permute-done.3.refs_1_ = f32[64,544]{1,0:T(8,128)S(1)} collective-permute-done((f32[64,544]{1,0:T(8,128)S(1)}, f32[64,544]{1,0:T(8,128)S(1)}, u32[]{:S(2)}, u32[]{:S(2)}) %collective-permute-start.3) | collective-permute-done | bytes 139296 | tf_op jit(solution)/shard_map/ppermute | solution.py:510
  25.0 5.3 %scan_ends.1 = (f32[64,2048]{1,0:T(8,128)}, bf16[24,2048]{1,0:T(8,128)(2,1)}, f32[64,16,128]{2,1,0:T(8,128)}, f32[64,16,128]{2,1,0:T(8,128)}) custom-call(f32[64,544]{1,0:T(8,128)} %copy-done.7, f32[64,544]{1,0:T(8,128)} %copy-done.11, bf16[512,2048]{1,0:T(8,128)(2,1)} %refs_2_.1, f32[1,2048]{1,0:T(1,128)} %bitcast.81, ...), custom_call_target="tpu_custom_call" | custom-call | tf_op jit(solution)/shard_map/scan_ends/pallas_call | solution.py:147
  30.3 3.8 %collective-permute-done.4.refs_5_ = bf16[640,512]{1,0:T(8,128)(2,1)S(1)} collective-permute-done((bf16[640,512]{1,0:T(8,128)(2,1)}, bf16[640,512]{1,0:T(8,128)(2,1)S(1)}, u32[]{:S(2)}, u32[]{:S(2)}) %collective-permute-start.4) | collective-permute-done | bytes 655392 | tf_op jit(solution)/shard_map/ppermute | solution.py:478
  35.6 2.7 %collective-permute-start.5 = (bf16[24,2048]{1,0:T(8,128)(2,1)}, bf16[24,2048]{1,0:T(8,128)(2,1)S(1)}, u32[]{:S(2)}, u32[]{:S(2)}) collective-permute-start(bf16[24,2048]{1,0:T(8,128)(2,1)} %get-tuple-element.46.refs_0_), channel_id=1, source_target_pairs={{8,0},{12,4},{16,8},{20,12},{24,16},{28,20},{0,24},{4,28},{9,1},{1... | collective-permute-start | bytes 294920 | tf_op jit(solution)/shard_map/ppermute | solution.py:470
  40.2 3.4 %collective-permute-done.5.refs_2_ = bf16[24,2048]{1,0:T(8,128)(2,1)S(1)} collective-permute-done((bf16[24,2048]{1,0:T(8,128)(2,1)}, bf16[24,2048]{1,0:T(8,128)(2,1)S(1)}, u32[]{:S(2)}, u32[]{:S(2)}) %collective-permute-start.5) | collective-permute-done | bytes 98336 | tf_op jit(solution)/shard_map/ppermute | solution.py:470
  45.2 5.5 %collective-permute-done.7.refs_4_ = bf16[24,2048]{1,0:T(8,128)(2,1)S(1)} collective-permute-done((bf16[24,2048]{1,0:T(8,128)(2,1)}, bf16[24,2048]{1,0:T(8,128)(2,1)S(1)}, u32[]{:S(2)}, u32[]{:S(2)}) %collective-permute-start.7) | collective-permute-done | bytes 98336 | tf_op jit(solution)/shard_map/ppermute | solution.py:470
  51.4 2.9 %collective-permute-done.11.refs_5_ = bf16[24,2048]{1,0:T(8,128)(2,1)} collective-permute-done((bf16[24,2048]{1,0:T(8,128)(2,1)S(1)}, bf16[24,2048]{1,0:T(8,128)(2,1)}, u32[]{:S(2)}, u32[]{:S(2)}) %collective-permute-start.11) | collective-permute-done | bytes 98336 | tf_op jit(solution)/shard_map/ppermute | solution.py:478
  56.3 5.8 %scan_mix.1.refs_0_ = bf16[64,2048]{1,0:T(8,128)(2,1)} custom-call(s32[1]{0:T(128)} %bitcast.15.z_place.z_ref, s32[1]{0:T(128)} %bitcast.16.x_place.x_ref, bf16[24,2048]{1,0:T(8,128)(2,1)} %get-tuple-element.46.refs_0_, bf16[24,2048]{1,0:T(8,128)(2,1)} %collective-permute-done.6.refs_1_, bf16[24,2048]{1,0:T(8,128)(2,1)} %copy-done.9, ...), custom_call_target="tpu_custom_call" | custom-call | tf_op jit(solution)/shard_map/scan_mix/pallas_call | solution.py:237
  74.2 9.0 %collective-permute-done.13.refs_2_ = bf16[64,2048]{1,0:T(8,128)(2,1)} collective-permute-done((bf16[64,2048]{1,0:T(8,128)(2,1)}, bf16[64,2048]{1,0:T(8,128)(2,1)}, u32[]{:S(2)}, u32[]{:S(2)}) %collective-permute-start.13) | collective-permute-done | bytes 262176 | tf_op jit(solution)/shard_map/ppermute | solution.py:470
  83.2 3.4 %collective-permute-done.15.refs_6_ = bf16[1408,512]{1,0:T(8,128)(2,1)S(1)} collective-permute-done((bf16[1408,512]{1,0:T(8,128)(2,1)}, bf16[1408,512]{1,0:T(8,128)(2,1)S(1)}, u32[]{:S(2)}, u32[]{:S(2)}) %collective-permute-start.15) | collective-permute-done | bytes 1441824 | tf_op jit(solution)/shard_map/ppermute | solution.py:478
  89.6 3.1 %out_product.1 = (bf16[272,1024]{1,0:T(8,128)(2,1)S(1)}, bf16[272,1024]{1,0:T(8,128)(2,1)S(1)}) custom-call(s32[1]{0:T(128)} %bitcast.15.z_place.z_ref, s32[1]{0:T(128)} %bitcast.16.x_place.x_ref, s32[1]{0:T(128)} %bitcast.27.e_ref, bf16[272,256]{1,0:T(8,128)(2,1)S(1)} %get-tuple-element.70.keep_pick_ref, ...), custom_call_target="tpu_custom_call" | custom-call | tf_op jit(solution)/shard_map/out_product/pallas_call | solution.py:299
  92.7 3.3 %collective-permute-start.16 = (bf16[272,1024]{1,0:T(8,128)(2,1)S(1)}, bf16[272,1024]{1,0:T(8,128)(2,1)S(1)}, u32[]{:S(2)}, u32[]{:S(2)}) collective-permute-start(bf16[272,1024]{1,0:T(8,128)(2,1)S(1)} %get-tuple-element.55), channel_id=1, source_target_pairs={{1,0},{0,1},{3,2},{2,3},{5,4},{4,5},{7,6},{6,7},{9,8},{8,9},{11,10... | collective-permute-start | bytes 1671176 | tf_op jit(solution)/shard_map/ppermute | solution.py:502
  97.8 7.9 %collective-permute-done.17 = bf16[136,1024]{1,0:T(8,128)(2,1)S(1)} collective-permute-done((bf16[136,1024]{1,0:T(8,128)(2,1)S(1)}, bf16[136,1024]{1,0:T(8,128)(2,1)S(1)}, u32[]{:S(2)}, u32[]{:S(2)}) %collective-permute-start.17) | collective-permute-done | bytes 278560 | tf_op jit(solution)/shard_map/ppermute | solution.py:510
  107.3 5.5 %collective-permute-done.19.refs_2_ = bf16[136,1024]{1,0:T(8,128)(2,1)S(1)} collective-permute-done((bf16[136,1024]{1,0:T(8,128)(2,1)S(1)}, bf16[136,1024]{1,0:T(8,128)(2,1)S(1)}, u32[]{:S(2)}, u32[]{:S(2)}) %collective-permute-start.19) | collective-permute-done | bytes 278560 | tf_op jit(solution)/shard_map/ppermute | solution.py:470
  113.5 5.4 %collective-permute-done.22.refs_6_ = bf16[136,1024]{1,0:T(8,128)(2,1)S(1)} collective-permute-done((bf16[136,1024]{1,0:T(8,128)(2,1)S(1)}, bf16[136,1024]{1,0:T(8,128)(2,1)S(1)}, u32[]{:S(2)}, u32[]{:S(2)}) %collective-permute-start.22) | collective-permute-done | bytes 278560 | tf_op jit(solution)/shard_map/ppermute | solution.py:470
  119.2 13.2 %collective-permute-done.21.refs_4_ = bf16[136,1024]{1,0:T(8,128)(2,1)S(1)} collective-permute-done((bf16[136,1024]{1,0:T(8,128)(2,1)S(1)}, bf16[136,1024]{1,0:T(8,128)(2,1)S(1)}, u32[]{:S(2)}, u32[]{:S(2)}) %collective-permute-start.21) | collective-permute-done | bytes 278560 | tf_op jit(solution)/shard_map/ppermute | solution.py:470
  132.8 7.4 %collective-permute-done.24.refs_5_ = bf16[136,1024]{1,0:T(8,128)(2,1)S(1)} collective-permute-done((bf16[136,1024]{1,0:T(8,128)(2,1)S(1)}, bf16[136,1024]{1,0:T(8,128)(2,1)S(1)}, u32[]{:S(2)}, u32[]{:S(2)}) %collective-permute-start.24) | collective-permute-done | bytes 278560 | tf_op jit(solution)/shard_map/ppermute | solution.py:478
  140.2 13.9 %expert_hidden.1.act_ref = bf16[288,1536]{1,0:T(8,128)(2,1)S(1)} custom-call(s32[1]{0:T(128)} %bitcast.15.z_place.z_ref, s32[1]{0:T(128)} %bitcast.16.x_place.x_ref, bf16[136,1024]{1,0:T(8,128)(2,1)S(1)} %fusion.4.refs_0_, bf16[136,1024]{1,0:T(8,128)(2,1)S(1)} %collective-permute-done.18.refs_1_, bf16[136,1024]{1,0:T(8,128)(2,1)S(1)} %collective-permute-done.19.refs_2_, ...), custom_call_target="tpu_custom_call" | custom-call | tf_op jit(solution)/shard_map/expert_hidden/pallas_call | solution.py:367
  154.1 2.9 %expert_down.5 = (bf16[136,1024]{1,0:T(8,128)(2,1)S(1)}, bf16[136,1024]{1,0:T(8,128)(2,1)S(1)}) custom-call(s32[1]{0:T(128)} %bitcast.16.x_place.x_ref, s32[1]{0:T(128)} %bitcast.31.blocks_ref, bf16[288,1536]{1,0:T(8,128)(2,1)S(1)} %expert_hidden.1.act_ref, bf16[1,1536,4096]{2,1,0:T(8,128)(2,1)} %weight_ref.7), custom_call_target="tpu_custom_call" | custom-call | tf_op jit(solution)/shard_map/expert_down/pallas_call | solution.py:408
  157.4 5.7 %expert_down.3 = (bf16[136,1024]{1,0:T(8,128)(2,1)S(1)}, bf16[136,1024]{1,0:T(8,128)(2,1)S(1)}, bf16[136,1024]{1,0:T(8,128)(2,1)S(1)}, bf16[136,1024]{1,0:T(8,128)(2,1)S(1)}) custom-call(s32[1]{0:T(128)} %bitcast.16.x_place.x_ref, s32[2]{0:T(128)S(1)} %pad_add_fusion.blocks_ref, bf16[288,1536]{1,0:T(8,128)(2,1)S(1)} %expert_hidden.1.act_ref, ...), custom_call_target="tpu_custom_call" | custom-call | tf_op jit(solution)/shard_map/expert_down/pallas_call | solution.py:408
  164.8 4.9 %collective-permute-done.25 = bf16[136,1024]{1,0:T(8,128)(2,1)S(1)} collective-permute-done((bf16[136,1024]{1,0:T(8,128)(2,1)S(1)}, bf16[136,1024]{1,0:T(8,128)(2,1)S(1)}, u32[]{:S(2)}, u32[]{:S(2)}) %collective-permute-start.25) | collective-permute-done | bytes 278560 | tf_op jit(solution)/shard_map/ppermute | solution.py:478
  169.8 2.9 %expert_down.4 = (bf16[136,1024]{1,0:T(8,128)(2,1)S(1)}, bf16[136,1024]{1,0:T(8,128)(2,1)S(1)}) custom-call(s32[1]{0:T(128)} %bitcast.16.x_place.x_ref, s32[1]{0:T(128)} %bitcast.26.blocks_ref, bf16[288,1536]{1,0:T(8,128)(2,1)S(1)} %expert_hidden.1.act_ref, bf16[1,1536,4096]{2,1,0:T(8,128)(2,1)} %weight_ref.7), custom_call_target="tpu_custom_call" | custom-call | tf_op jit(solution)/shard_map/expert_down/pallas_call | solution.py:408
  172.7 2.9 %collective-permute-done.30 = bf16[136,1024]{1,0:T(8,128)(2,1)S(1)} collective-permute-done((bf16[136,1024]{1,0:T(8,128)(2,1)S(1)}, bf16[136,1024]{1,0:T(8,128)(2,1)S(1)}, u32[]{:S(2)}, u32[]{:S(2)}) %collective-permute-start.30) | collective-permute-done | bytes 278560 | tf_op jit(solution)/shard_map/ppermute | solution.py:478
  175.7 2.3 %collective-permute-start.31 = (bf16[136,1024]{1,0:T(8,128)(2,1)S(1)}, bf16[136,1024]{1,0:T(8,128)(2,1)S(1)}, u32[]{:S(2)}, u32[]{:S(2)}) collective-permute-start(bf16[136,1024]{1,0:T(8,128)(2,1)S(1)} %add_convert_fusion.2), channel_id=1, source_target_pairs={{8,0},{12,4},{16,8},{20,12},{24,16},{28,20},{0,24},{4,28},{9,1},{1... | collective-permute-start | bytes 835592 | tf_op jit(solution)/shard_map/ppermute | solution.py:470
  178.1 8.1 %collective-permute-done.27 = bf16[136,1024]{1,0:T(8,128)(2,1)S(1)} collective-permute-done((bf16[136,1024]{1,0:T(8,128)(2,1)S(1)}, bf16[136,1024]{1,0:T(8,128)(2,1)S(1)}, u32[]{:S(2)}, u32[]{:S(2)}) %collective-permute-start.27) | collective-permute-done | bytes 278560 | tf_op jit(solution)/shard_map/ppermute | solution.py:470
  187.2 4.8 %collective-permute-done.31 = bf16[136,1024]{1,0:T(8,128)(2,1)S(1)} collective-permute-done((bf16[136,1024]{1,0:T(8,128)(2,1)S(1)}, bf16[136,1024]{1,0:T(8,128)(2,1)S(1)}, u32[]{:S(2)}, u32[]{:S(2)}) %collective-permute-start.31) | collective-permute-done | bytes 278560 | tf_op jit(solution)/shard_map/ppermute | solution.py:470
  196.4 5.8 %collective-permute-start.32 = (bf16[34,1024]{1,0:T(8,128)(2,1)S(1)}, bf16[34,1024]{1,0:T(8,128)(2,1)S(1)}, u32[]{:S(2)}, u32[]{:S(2)}) collective-permute-start(bf16[34,1024]{1,0:T(8,128)(2,1)S(1)} %get-tuple-element.71), channel_id=1, source_target_pairs={{0,0},{8,1},{16,2},{24,3},{4,4},{12,5},{20,6},{28,7},{1,8},{9,9},{... | collective-permute-start | bytes 208904 | tf_op jit(solution)/shard_map/ppermute | solution.py:656
  202.3 2.5 %collective-permute-done.32 = bf16[34,1024]{1,0:T(8,128)(2,1)S(1)} collective-permute-done((bf16[34,1024]{1,0:T(8,128)(2,1)S(1)}, bf16[34,1024]{1,0:T(8,128)(2,1)S(1)}, u32[]{:S(2)}, u32[]{:S(2)}) %collective-permute-start.32) | collective-permute-done | bytes 69664 | tf_op jit(solution)/shard_map/ppermute | solution.py:656
  (153 shorter events, 43.7 us)
Async XLA Ops:
  0.0 15.1 %collective-permute-start.1 = (bf16[64,1024]{1,0:T(8,128)(2,1)}, bf16[64,1024]{1,0:T(8,128)(2,1)S(1)}, u32[]{:S(2)}, u32[]{:S(2)}) collective-permute-start(bf16[64,1024]{1,0:T(8,128)(2,1)} %param.27), channel_id=1, source_target_pairs={{0,0},{8,1},{16,2},{24,3},{4,4},{12,5},{20,6},{28,7},{1,8},{9,9},{... | collective-permute-start | bytes 393224 | tf_op jit(solution)/shard_map/ppermute | solution.py:524
  16.8 17.3 %collective-permute-start.4 = (bf16[640,512]{1,0:T(8,128)(2,1)}, bf16[640,512]{1,0:T(8,128)(2,1)S(1)}, u32[]{:S(2)}, u32[]{:S(2)}) collective-permute-start(bf16[640,512]{1,0:T(8,128)(2,1)} %slice.49), channel_id=1, source_target_pairs={{4,0},{0,4},{12,8},{8,12},{20,16},{16,20},{28,24},{24,28},{5,1},{1... | collective-permute-start | bytes 1966088 | tf_op jit(solution)/shard_map/ppermute | solution.py:478
  19.1 5.3 %collective-permute-start.3 = (f32[64,544]{1,0:T(8,128)S(1)}, f32[64,544]{1,0:T(8,128)S(1)}, u32[]{:S(2)}, u32[]{:S(2)}) collective-permute-start(f32[64,544]{1,0:T(8,128)S(1)} %add.242.refs_0_), channel_id=1, source_target_pairs={{2,0},{3,1},{0,2},{1,3},{6,4},{7,5},{4,6},{5,7},{10,8},{11,9},{8,1... | collective-permute-start | bytes 417800 | tf_op jit(solution)/shard_map/ppermute | solution.py:510
  35.0 8.9 %collective-permute-start.8 = (bf16[24,2048]{1,0:T(8,128)(2,1)}, bf16[24,2048]{1,0:T(8,128)(2,1)S(1)}, u32[]{:S(2)}, u32[]{:S(2)}) collective-permute-start(bf16[24,2048]{1,0:T(8,128)(2,1)} %get-tuple-element.46.refs_0_), channel_id=1, source_target_pairs={{24,0},{28,4},{0,8},{4,12},{8,16},{12,20},{16,24},{20,28},{25,1},{... | collective-permute-start | bytes 294920 | tf_op jit(solution)/shard_map/ppermute | solution.py:470
  35.6 8.1 %collective-permute-start.5 = (bf16[24,2048]{1,0:T(8,128)(2,1)}, bf16[24,2048]{1,0:T(8,128)(2,1)S(1)}, u32[]{:S(2)}, u32[]{:S(2)}) collective-permute-start(bf16[24,2048]{1,0:T(8,128)(2,1)} %get-tuple-element.46.refs_0_), channel_id=1, source_target_pairs={{8,0},{12,4},{16,8},{20,12},{24,16},{28,20},{0,24},{4,28},{9,1},{1... | collective-permute-start | bytes 294920 | tf_op jit(solution)/shard_map/ppermute | solution.py:470
  38.3 5.3 %collective-permute-start.6 = (bf16[24,2048]{1,0:T(8,128)(2,1)}, bf16[24,2048]{1,0:T(8,128)(2,1)}, u32[]{:S(2)}, u32[]{:S(2)}) collective-permute-start(bf16[24,2048]{1,0:T(8,128)(2,1)} %get-tuple-element.46.refs_0_), channel_id=1, source_target_pairs={{4,0},{0,4},{12,8},{8,12},{20,16},{16,20},{28,24},{24,28},{5,1},{1... | collective-permute-start | bytes 294920 | tf_op jit(solution)/shard_map/ppermute | solution.py:478
  43.6 7.1 %collective-permute-start.7 = (bf16[24,2048]{1,0:T(8,128)(2,1)}, bf16[24,2048]{1,0:T(8,128)(2,1)S(1)}, u32[]{:S(2)}, u32[]{:S(2)}) collective-permute-start(bf16[24,2048]{1,0:T(8,128)(2,1)} %get-tuple-element.46.refs_0_), channel_id=1, source_target_pairs={{16,0},{20,4},{24,8},{28,12},{0,16},{4,20},{8,24},{12,28},{17,1},{... | collective-permute-start | bytes 294920 | tf_op jit(solution)/shard_map/ppermute | solution.py:470
  43.6 7.1 %collective-permute-start.9 = (bf16[24,2048]{1,0:T(8,128)(2,1)S(1)}, bf16[24,2048]{1,0:T(8,128)(2,1)S(1)}, u32[]{:S(2)}, u32[]{:S(2)}) collective-permute-start(bf16[24,2048]{1,0:T(8,128)(2,1)S(1)} %collective-permute-done.5.refs_2_), channel_id=1, source_target_pairs={{4,0},{0,4},{12,8},{8,12},{20,16},{16,20},{28,24},{24,28},{5,1},{1... | collective-permute-start | bytes 294920 | tf_op jit(solution)/shard_map/ppermute | solution.py:478
  43.9 6.8 %collective-permute-start.10 = (bf16[24,2048]{1,0:T(8,128)(2,1)S(1)}, bf16[24,2048]{1,0:T(8,128)(2,1)S(1)}, u32[]{:S(2)}, u32[]{:S(2)}) collective-permute-start(bf16[24,2048]{1,0:T(8,128)(2,1)S(1)} %collective-permute-done.8.refs_6_), channel_id=1, source_target_pairs={{4,0},{0,4},{12,8},{8,12},{20,16},{16,20},{28,24},{24,28},{5,1},{1... | collective-permute-start | bytes 294920 | tf_op jit(solution)/shard_map/ppermute | solution.py:478
  55.6 31.0 %collective-permute-start.15 = (bf16[1408,512]{1,0:T(8,128)(2,1)}, bf16[1408,512]{1,0:T(8,128)(2,1)S(1)}, u32[]{:S(2)}, u32[]{:S(2)}) collective-permute-start(bf16[1408,512]{1,0:T(8,128)(2,1)} %slice.59), channel_id=1, source_target_pairs={{4,0},{0,4},{12,8},{8,12},{20,16},{16,20},{28,24},{24,28},{5,1},{1... | collective-permute-start | bytes 4325384 | tf_op jit(solution)/shard_map/ppermute | solution.py:478
  62.1 12.0 %collective-permute-start.12 = (bf16[64,2048]{1,0:T(8,128)(2,1)}, bf16[64,2048]{1,0:T(8,128)(2,1)}, u32[]{:S(2)}, u32[]{:S(2)}) collective-permute-start(bf16[64,2048]{1,0:T(8,128)(2,1)} %scan_mix.1.refs_0_), channel_id=1, source_target_pairs={{8,0},{12,4},{16,8},{20,12},{24,16},{28,20},{0,24},{4,28},{9,1},{1... | collective-permute-start | bytes 786440 | tf_op jit(solution)/shard_map/ppermute | solution.py:470
  63.3 19.9 %collective-permute-start.13 = (bf16[64,2048]{1,0:T(8,128)(2,1)}, bf16[64,2048]{1,0:T(8,128)(2,1)}, u32[]{:S(2)}, u32[]{:S(2)}) collective-permute-start(bf16[64,2048]{1,0:T(8,128)(2,1)} %scan_mix.1.refs_0_), channel_id=1, source_target_pairs={{16,0},{20,4},{24,8},{28,12},{0,16},{4,20},{8,24},{12,28},{17,1},{... | collective-permute-start | bytes 786440 | tf_op jit(solution)/shard_map/ppermute | solution.py:470
  63.3 19.9 %collective-permute-start.14 = (bf16[64,2048]{1,0:T(8,128)(2,1)}, bf16[64,2048]{1,0:T(8,128)(2,1)}, u32[]{:S(2)}, u32[]{:S(2)}) collective-permute-start(bf16[64,2048]{1,0:T(8,128)(2,1)} %scan_mix.1.refs_0_), channel_id=1, source_target_pairs={{24,0},{28,4},{0,8},{4,12},{8,16},{12,20},{16,24},{20,28},{25,1},{... | collective-permute-start | bytes 786440 | tf_op jit(solution)/shard_map/ppermute | solution.py:470
  97.8 7.9 %collective-permute-start.17 = (bf16[136,1024]{1,0:T(8,128)(2,1)S(1)}, bf16[136,1024]{1,0:T(8,128)(2,1)S(1)}, u32[]{:S(2)}, u32[]{:S(2)}) collective-permute-start(bf16[136,1024]{1,0:T(8,128)(2,1)S(1)} %slice.92), channel_id=1, source_target_pairs={{2,0},{3,1},{0,2},{1,3},{6,4},{7,5},{4,6},{5,7},{10,8},{11,9},{8,1... | collective-permute-start | bytes 835592 | tf_op jit(solution)/shard_map/ppermute | solution.py:510
  105.8 7.0 %collective-permute-start.19 = (bf16[136,1024]{1,0:T(8,128)(2,1)S(1)}, bf16[136,1024]{1,0:T(8,128)(2,1)S(1)}, u32[]{:S(2)}, u32[]{:S(2)}) collective-permute-start(bf16[136,1024]{1,0:T(8,128)(2,1)S(1)} %fusion.4.refs_0_), channel_id=1, source_target_pairs={{8,0},{12,4},{16,8},{20,12},{24,16},{28,20},{0,24},{4,28},{9,1},{1... | collective-permute-start | bytes 835592 | tf_op jit(solution)/shard_map/ppermute | solution.py:470
  105.8 7.0 %collective-permute-start.18 = (bf16[136,1024]{1,0:T(8,128)(2,1)S(1)}, bf16[136,1024]{1,0:T(8,128)(2,1)S(1)}, u32[]{:S(2)}, u32[]{:S(2)}) collective-permute-start(bf16[136,1024]{1,0:T(8,128)(2,1)S(1)} %fusion.4.refs_0_), channel_id=1, source_target_pairs={{4,0},{0,4},{12,8},{8,12},{20,16},{16,20},{28,24},{24,28},{5,1},{1... | collective-permute-start | bytes 835592 | tf_op jit(solution)/shard_map/ppermute | solution.py:478
  106.7 12.2 %collective-permute-start.22 = (bf16[136,1024]{1,0:T(8,128)(2,1)S(1)}, bf16[136,1024]{1,0:T(8,128)(2,1)S(1)}, u32[]{:S(2)}, u32[]{:S(2)}) collective-permute-start(bf16[136,1024]{1,0:T(8,128)(2,1)S(1)} %fusion.4.refs_0_), channel_id=1, source_target_pairs={{24,0},{28,4},{0,8},{4,12},{8,16},{12,20},{16,24},{20,28},{25,1},{... | collective-permute-start | bytes 835592 | tf_op jit(solution)/shard_map/ppermute | solution.py:470
  112.8 6.4 %collective-permute-start.20 = (bf16[136,1024]{1,0:T(8,128)(2,1)S(1)}, bf16[136,1024]{1,0:T(8,128)(2,1)S(1)}, u32[]{:S(2)}, u32[]{:S(2)}) collective-permute-start(bf16[136,1024]{1,0:T(8,128)(2,1)S(1)} %collective-permute-done.19.refs_2_), channel_id=1, source_target_pairs={{4,0},{0,4},{12,8},{8,12},{20,16},{16,20},{28,24},{24,28},{5,1},{1... | collective-permute-start | bytes 835592 | tf_op jit(solution)/shard_map/ppermute | solution.py:478
  112.8 19.6 %collective-permute-start.21 = (bf16[136,1024]{1,0:T(8,128)(2,1)S(1)}, bf16[136,1024]{1,0:T(8,128)(2,1)S(1)}, u32[]{:S(2)}, u32[]{:S(2)}) collective-permute-start(bf16[136,1024]{1,0:T(8,128)(2,1)S(1)} %fusion.4.refs_0_), channel_id=1, source_target_pairs={{16,0},{20,4},{24,8},{28,12},{0,16},{4,20},{8,24},{12,28},{17,1},{... | collective-permute-start | bytes 835592 | tf_op jit(solution)/shard_map/ppermute | solution.py:470
  118.9 13.5 %collective-permute-start.23 = (bf16[136,1024]{1,0:T(8,128)(2,1)S(1)}, bf16[136,1024]{1,0:T(8,128)(2,1)S(1)}, u32[]{:S(2)}, u32[]{:S(2)}) collective-permute-start(bf16[136,1024]{1,0:T(8,128)(2,1)S(1)} %collective-permute-done.22.refs_6_), channel_id=1, source_target_pairs={{4,0},{0,4},{12,8},{8,12},{20,16},{16,20},{28,24},{24,28},{5,1},{1... | collective-permute-start | bytes 835592 | tf_op jit(solution)/shard_map/ppermute | solution.py:478
  132.4 7.7 %collective-permute-start.24 = (bf16[136,1024]{1,0:T(8,128)(2,1)S(1)}, bf16[136,1024]{1,0:T(8,128)(2,1)S(1)}, u32[]{:S(2)}, u32[]{:S(2)}) collective-permute-start(bf16[136,1024]{1,0:T(8,128)(2,1)S(1)} %collective-permute-done.21.refs_4_), channel_id=1, source_target_pairs={{4,0},{0,4},{12,8},{8,12},{20,16},{16,20},{28,24},{24,28},{5,1},{1... | collective-permute-start | bytes 835592 | tf_op jit(solution)/shard_map/ppermute | solution.py:478
  156.9 7.4 %collective-permute-start.26 = (bf16[136,1024]{1,0:T(8,128)(2,1)S(1)}, bf16[136,1024]{1,0:T(8,128)(2,1)S(1)}, u32[]{:S(2)}, u32[]{:S(2)}) collective-permute-start(bf16[136,1024]{1,0:T(8,128)(2,1)S(1)} %get-tuple-element.63), channel_id=1, source_target_pairs={{4,0},{0,4},{12,8},{8,12},{20,16},{16,20},{28,24},{24,28},{5,1},{1... | collective-permute-start | bytes 835592 | tf_op jit(solution)/shard_map/ppermute | solution.py:478
  163.1 6.6 %collective-permute-start.25 = (bf16[136,1024]{1,0:T(8,128)(2,1)S(1)}, bf16[136,1024]{1,0:T(8,128)(2,1)S(1)}, u32[]{:S(2)}, u32[]{:S(2)}) collective-permute-start(bf16[136,1024]{1,0:T(8,128)(2,1)S(1)} %get-tuple-element.58), channel_id=1, source_target_pairs={{4,0},{0,4},{12,8},{8,12},{20,16},{16,20},{28,24},{24,28},{5,1},{1... | collective-permute-start | bytes 835592 | tf_op jit(solution)/shard_map/ppermute | solution.py:478
  164.3 11.3 %collective-permute-start.30 = (bf16[136,1024]{1,0:T(8,128)(2,1)S(1)}, bf16[136,1024]{1,0:T(8,128)(2,1)S(1)}, u32[]{:S(2)}, u32[]{:S(2)}) collective-permute-start(bf16[136,1024]{1,0:T(8,128)(2,1)S(1)} %get-tuple-element.68), channel_id=1, source_target_pairs={{4,0},{0,4},{12,8},{8,12},{20,16},{16,20},{28,24},{24,28},{5,1},{1... | collective-permute-start | bytes 835592 | tf_op jit(solution)/shard_map/ppermute | solution.py:478
  164.7 21.4 %collective-permute-start.27 = (bf16[136,1024]{1,0:T(8,128)(2,1)S(1)}, bf16[136,1024]{1,0:T(8,128)(2,1)S(1)}, u32[]{:S(2)}, u32[]{:S(2)}) collective-permute-start(bf16[136,1024]{1,0:T(8,128)(2,1)S(1)} %add_convert_fusion.4), channel_id=1, source_target_pairs={{16,0},{20,4},{24,8},{28,12},{0,16},{4,20},{8,24},{12,28},{17,1},{... | collective-permute-start | bytes 835592 | tf_op jit(solution)/shard_map/ppermute | solution.py:470
  169.8 17.5 %collective-permute-start.29 = (bf16[136,1024]{1,0:T(8,128)(2,1)S(1)}, bf16[136,1024]{1,0:T(8,128)(2,1)S(1)}, u32[]{:S(2)}, u32[]{:S(2)}) collective-permute-start(bf16[136,1024]{1,0:T(8,128)(2,1)S(1)} %add_convert_fusion.3), channel_id=1, source_target_pairs={{24,0},{28,4},{0,8},{4,12},{8,16},{12,20},{16,24},{20,28},{25,1},{... | collective-permute-start | bytes 835592 | tf_op jit(solution)/shard_map/ppermute | solution.py:470
  175.7 16.3 %collective-permute-start.31 = (bf16[136,1024]{1,0:T(8,128)(2,1)S(1)}, bf16[136,1024]{1,0:T(8,128)(2,1)S(1)}, u32[]{:S(2)}, u32[]{:S(2)}) collective-permute-start(bf16[136,1024]{1,0:T(8,128)(2,1)S(1)} %add_convert_fusion.2), channel_id=1, source_target_pairs={{8,0},{12,4},{16,8},{20,12},{24,16},{28,20},{0,24},{4,28},{9,1},{1... | collective-permute-start | bytes 835592 | tf_op jit(solution)/shard_map/ppermute | solution.py:470
  186.1 7.6 %collective-permute-start.28 = (bf16[136,1024]{1,0:T(8,128)(2,1)S(1)}, bf16[136,1024]{1,0:T(8,128)(2,1)S(1)}, u32[]{:S(2)}, u32[]{:S(2)}) collective-permute-start(bf16[136,1024]{1,0:T(8,128)(2,1)S(1)} %get-tuple-element.64), channel_id=1, source_target_pairs={{4,0},{0,4},{12,8},{8,12},{20,16},{16,20},{28,24},{24,28},{5,1},{1... | collective-permute-start | bytes 835592 | tf_op jit(solution)/shard_map/ppermute | solution.py:478
  194.2 8.1 %collective-permute-start.35 = (bf16[34,1024]{1,0:T(8,128)(2,1)S(1)}, bf16[34,1024]{1,0:T(8,128)(2,1)S(1)}, u32[]{:S(2)}, u32[]{:S(2)}) collective-permute-start(bf16[34,1024]{1,0:T(8,128)(2,1)S(1)} %get-tuple-element.72), channel_id=1, source_target_pairs={{3,0},{11,1},{19,2},{27,3},{7,4},{15,5},{23,6},{31,7},{0,8},{8,9},... | collective-permute-start | bytes 208904 | tf_op jit(solution)/shard_map/ppermute | solution.py:656
  195.9 6.4 %collective-permute-start.34 = (bf16[34,1024]{1,0:T(8,128)(2,1)S(1)}, bf16[34,1024]{1,0:T(8,128)(2,1)S(1)}, u32[]{:S(2)}, u32[]{:S(2)}) collective-permute-start(bf16[34,1024]{1,0:T(8,128)(2,1)S(1)} %get-tuple-element.73), channel_id=1, source_target_pairs={{2,0},{10,1},{18,2},{26,3},{6,4},{14,5},{22,6},{30,7},{3,8},{11,9}... | collective-permute-start | bytes 208904 | tf_op jit(solution)/shard_map/ppermute | solution.py:656
  195.9 6.4 %collective-permute-start.33 = (bf16[34,1024]{1,0:T(8,128)(2,1)S(1)}, bf16[34,1024]{1,0:T(8,128)(2,1)S(1)}, u32[]{:S(2)}, u32[]{:S(2)}) collective-permute-start(bf16[34,1024]{1,0:T(8,128)(2,1)S(1)} %get-tuple-element.74), channel_id=1, source_target_pairs={{1,0},{9,1},{17,2},{25,3},{5,4},{13,5},{21,6},{29,7},{2,8},{10,9},... | collective-permute-start | bytes 208904 | tf_op jit(solution)/shard_map/ppermute | solution.py:656
  196.4 8.4 %collective-permute-start.32 = (bf16[34,1024]{1,0:T(8,128)(2,1)S(1)}, bf16[34,1024]{1,0:T(8,128)(2,1)S(1)}, u32[]{:S(2)}, u32[]{:S(2)}) collective-permute-start(bf16[34,1024]{1,0:T(8,128)(2,1)S(1)} %get-tuple-element.71), channel_id=1, source_target_pairs={{0,0},{8,1},{16,2},{24,3},{4,4},{12,5},{20,6},{28,7},{1,8},{9,9},{... | collective-permute-start | bytes 208904 | tf_op jit(solution)/shard_map/ppermute | solution.py:656
  (27 other events, 154.8 us)
where the time goes:
time: 208 us; the launch traced here: 206 us
  waiting for transfers between devices  97.6 us (47%)
  Pallas kernels  43.2 us (21%)
  starting transfers between devices  38.6 us (19%)
  local copies, waits for them, and re-layouts  17.2 us (8%)
  other arithmetic  6.72 us (3%)
    ppermute x12, waiting for transfers between devices, from_z(): return lax.ppermute(block, 'seq', pairs)  54.9 us
    ppermute x14, waiting for transfers between devices, from_x(): return lax.ppermute(block, 'seq', pairs)  27.2 us
    pallas_call x1, Pallas kernels, expert_hidden(): pl.pallas_call(functools.partial(hidden_kernel, z_count, x_count), grid=(...  13.9 us
    pallas_call x3, Pallas kernels, expert_down(): pl.pallas_call(functools.partial(down_kernel, x_count), grid_spec=pltpu.P...  11.4 us
    ppermute x2, waiting for transfers between devices, from_y(): return lax.ppermute(block, 'exp', pairs)  10.3 us
    ppermute x12, starting transfers between devices, from_z(): return lax.ppermute(block, 'seq', pairs)  9.09 us
    ppermute x14, starting transfers between devices, from_x(): return lax.ppermute(block, 'seq', pairs)  8.94 us
    ppermute x4, starting transfers between devices, per_device(): back.append(lax.ppermute(piece, ('seq', 'exp'), pairs))  8.02 us
  transfers between devices with their start and end apart: 36, of which 21 were waited for; matrix products, arithmetic and copies ran while one was open for 8% of the time, Pallas kernels for 11%

commit v1 on v0

--- a/solution.py
+++ b/solution.py
@@ -90,7 +90,7 @@
 def ends_kernel(count, *refs):
     parts = refs[:count]
     proj_ref, bias_ref, rate_ref, x_ref, info_ref = refs[count : count + 5]
-    size_ref, load_ref, b_ref, c_ref, low_ref, drive_ref = refs[count + 5 :]
+    size_ref, load_ref, both_ref, b_ref, low_ref, drive_ref = refs[count + 5 :]
     rows, width = x_ref.shape
     states = rate_ref.shape[0]
     low_rank = low_ref.shape[1]
@@ -102,10 +102,9 @@
         for part in parts[1:]:
             total = total + part[...]
         low_ref[...] = total[:, :low_rank].astype(jnp.bfloat16)
+        both_ref[...] = total[:, low_rank : low_rank + 2 * states]
         b_mat = total[:, low_rank : low_rank + states]
-        c_mat = total[:, low_rank + states : low_rank + 2 * states]
         b_ref[...] = jnp.broadcast_to(b_mat[:, :, None], b_ref.shape)
-        c_ref[...] = jnp.broadcast_to(c_mat[:, :, None], c_ref.shape)
 
     size = softplus(
         jnp.dot(low_ref[...], proj_ref[...], preferred_element_type=jnp.float32) + bias_ref[...]
@@ -143,7 +142,6 @@
     states = rates.shape[0]
     width = tile_of(channels, 1024)
     load_rows = -(-(states + 2) // 8) * 8
-    wide = jax.ShapeDtypeStruct((rows, states, 128), jnp.float32)
     return pl.pallas_call(
         functools.partial(ends_kernel, len(partials)),
         grid=(channels // width,),
@@ -158,16 +156,15 @@
         out_specs=[
             pl.BlockSpec((rows, width), lambda i: (0, i)),
             pl.BlockSpec((load_rows, width), lambda i: (0, i)),
-            pl.BlockSpec(wide.shape, lambda i: (0, 0, 0)),
-            pl.BlockSpec(wide.shape, lambda i: (0, 0, 0)),
+            pl.BlockSpec((rows, 2 * states), lambda i: (0, 0)),
         ],
         out_shape=[
             jax.ShapeDtypeStruct((rows, channels), jnp.float32),
             jax.ShapeDtypeStruct((load_rows, channels), jnp.bfloat16),
-            wide,
-            wide,
+            jax.ShapeDtypeStruct((rows, 2 * states), jnp.float32),
         ],
         scratch_shapes=[
+            pltpu.VMEM((rows, states, 128), jnp.float32),
             pltpu.VMEM((rows, dt_proj.shape[0]), jnp.bfloat16),
             pltpu.VMEM((rows, width), jnp.float32),
         ],
@@ -178,8 +175,8 @@
 def mix_kernel(z_count, x_count, z_place, x_place, *refs):
     count = z_count * x_count
     loads = refs[:count]
-    size_ref, x_ref, z_ref, b_ref, c_ref, rate_ref, skip_ref, out_ref = refs[count : count + 8]
-    drive_ref, y_ref, load_ref = refs[count + 8 :]
+    size_ref, x_ref, z_ref, both_ref, rate_ref, skip_ref, out_ref = refs[count : count + 7]
+    drive_ref, y_ref, load_ref, b_ref, c_ref = refs[count + 7 :]
     across = lanes_of(x_ref.shape[1])
     for k in range(count):
         z_from = lax.rem(z_place[0] + k // x_count, z_count)
@@ -188,6 +185,13 @@
     rows, width = x_ref.shape
     states = rate_ref.shape[0]
     groups = width // 128
+
+    @pl.when(pl.program_id(0) == 0)
+    def _():
+        both = both_ref[...]
+        b_ref[...] = jnp.broadcast_to(both[:, :states, None], b_ref.shape)
+        c_ref[...] = jnp.broadcast_to(both[:, states:, None], c_ref.shape)
+
     rates = rate_ref[...]
     x_f = x_ref[...].astype(jnp.float32)
     drive_ref[...] = size_ref[...] * x_f
@@ -225,7 +229,7 @@
     out_ref[...] = (scanned * (z_f / (1.0 + jnp.exp(-z_f)))).astype(jnp.bfloat16)
 
 
-def scan_mix(z_at, x_at, loads, step_size, xconv, z_in, b_wide, c_wide, rates, d_skip):
+def scan_mix(z_at, x_at, loads, step_size, xconv, z_in, both, rates, d_skip):
     rows, channels = xconv.shape
     states = rates.shape[0]
     width = tile_of(channels, 1024)
@@ -244,17 +248,17 @@
             by_lane(rows),
             by_lane(rows),
             by_lane(rows),
-            pl.BlockSpec(b_wide.shape, lambda i: (0, 0, 0)),
-            pl.BlockSpec(c_wide.shape, lambda i: (0, 0, 0)),
+            pl.BlockSpec(both.shape, lambda i: (0, 0)),
             by_lane(states),
             by_lane(1),
         ],
         out_specs=by_lane(rows),
         out_shape=jax.ShapeDtypeStruct((rows, channels), jnp.bfloat16),
         scratch_shapes=[pltpu.VMEM((rows, width), jnp.float32)] * 2
-        + [pltpu.VMEM((len(flat), flat[0].shape[0], width), jnp.float32)],
+        + [pltpu.VMEM((len(flat), flat[0].shape[0], width), jnp.float32)]
+        + [pltpu.VMEM((rows, states, 128), jnp.float32)] * 2,
         name="scan_mix",
-    )(z_at, x_at, *flat, step_size, xconv, z_in, b_wide, c_wide, rates, d_skip)
+    )(z_at, x_at, *flat, step_size, xconv, z_in, both, rates, d_skip)
 
 
 def out_kernel(z_count, counts, z_ref, x_ref, e_ref, keep_pick_ref, send_pick_ref, resid_ref, *refs):
@@ -479,14 +483,14 @@
 
     turns = sorted(range(1, z_count), key=lambda r: min(r, z_count - r))
 
-    def gathered(block):
+    def gathered(block, chained=True):
         rows = {(0, 0): block}
         others = range(1, x_count)
         for i in others:
             rows[0, i] = from_x(block, i)
         sent = block
         for k, r in enumerate(turns):
-            if k >= 2:
+            if chained and k >= 2:
                 sent = after(sent, rows[turns[k - 2], 0], *[rows[0, i] for i in others])
             rows[r, 0] = from_z(sent, r)
         for k, r in enumerate(turns):
@@ -556,13 +560,13 @@
     cut = channels * 5 // 16
     uppers = [from_x(after(out_proj, halo)[:cut], i) for i in range(1, x_count)]
     partials = [chip_sum] + [from_y(chip_sum, r) for r in range(1, y_count)]
-    step_size, load, b_wide, c_wide = scan_ends(partials, dt_proj, dt_bias[None], rates, xconv, info)
-    loads = gathered(after(load, resid_here, *uppers))
+    step_size, load, both = scan_ends(partials, dt_proj, dt_bias[None], rates, xconv, info)
+    loads = gathered(after(load, resid_here, *uppers), False)
     held_proj = after(out_proj, *[part for pair in loads for part in pair])
     lowers = [from_x(held_proj[cut:], i) for i in range(1, x_count)]
     columns = [[out_proj]] + [list(pair) for pair in zip(uppers, lowers)]
     mixed = scan_mix(
-        z_one, x_one, loads, step_size, xconv, z_in, b_wide, c_wide, rates, d_skip[None]
+        z_one, x_one, loads, step_size, xconv, z_in, both, rates, d_skip[None]
     )
     along_z = [mixed] + [from_z(mixed, r) for r in range(1, z_count)]
 

time: 208 us -> 208 us (level)
  starting transfers between devices: 38.6 us -> 59.6 us
  waiting for transfers between devices: 97.6 us -> 77 us
    ppermute x12, waiting for transfers between devices: 54.9 us -> 37.2 us  [from_z(): return lax.ppermute(block, 'seq', pairs)]
    ppermute x4, starting transfers between devices: 8.02 us -> 21 us  [per_device(): back.append(lax.ppermute(piece, ('seq', 'exp'), pairs))]
    ppermute x12, starting transfers between devices: 9.09 us -> 17.3 us  [from_z(): return lax.ppermute(block, 'seq', pairs)]
    ppermute x14, waiting for transfers between devices: 27.2 us -> 24.8 us  [from_x(): return lax.ppermute(block, 'seq', pairs)]
  transfers between devices with their start and end apart: 36 -> 36, of which waited for: 21 -> 19; matrix products, arithmetic and copies ran while one was open for 8% -> 8% of each run, Pallas kernels for 11% -> 11%
where the time goes in v1:
time: 208 us; the launch traced here: 206 us
  waiting for transfers between devices  77 us (37%)
  starting transfers between devices  59.6 us (29%)
  Pallas kernels  42.7 us (21%)
  local copies, waits for them, and re-layouts  17.1 us (8%)
  other arithmetic  6.72 us (3%)
    ppermute x12, waiting for transfers between devices, from_z(): return lax.ppermute(block, 'seq', pairs)  37.2 us
    ppermute x14, waiting for transfers between devices, from_x(): return lax.ppermute(block, 'seq', pairs)  24.8 us
    ppermute x4, starting transfers between devices, per_device(): back.append(lax.ppermute(piece, ('seq', 'exp'), pairs))  21 us
    ppermute x12, starting transfers between devices, from_z(): return lax.ppermute(block, 'seq', pairs)  17.3 us
    pallas_call x1, Pallas kernels, expert_hidden(): pl.pallas_call(functools.partial(hidden_kernel, z_count, x_count), grid=(...  13.9 us
    pallas_call x3, Pallas kernels, expert_down(): pl.pallas_call(functools.partial(down_kernel, x_count), grid_spec=pltpu.P...  11.5 us
    ppermute x2, waiting for transfers between devices, from_y(): return lax.ppermute(block, 'exp', pairs)  10.3 us
    ppermute x14, starting transfers between devices, from_x(): return lax.ppermute(block, 'seq', pairs)  9.36 us
  transfers between devices with their start and end apart: 36, of which 19 were waited for; matrix products, arithmetic and copies ran while one was open for 8% of the time, Pallas kernels for 11%

profile of v1, /device:TPU:5, one launch (start us, length us, event | category | flops | bytes accessed | tf_op | source)
XLA Modules:
  0.0 205.7 jit_solution(4841041415889186035)
XLA Ops:
  0.0 5.9 %collective-permute-start.1 = (bf16[64,1024]{1,0:T(8,128)(2,1)}, bf16[64,1024]{1,0:T(8,128)(2,1)S(1)}, u32[]{:S(2)}, u32[]{:S(2)}) collective-permute-start(bf16[64,1024]{1,0:T(8,128)(2,1)} %param.27), channel_id=1, source_target_pairs={{0,0},{8,1},{16,2},{24,3},{4,4},{12,5},{20,6},{28,7},{1,8},{9,9},{... | collective-permute-start | bytes 393224 | tf_op jit(solution)/shard_map/ppermute | solution.py:528
  6.6 3.1 %collective-permute-start = (bf16[8,2048]{1,0:T(8,128)(2,1)S(1)}, bf16[8,2048]{1,0:T(8,128)(2,1)S(1)}, u32[]{:S(2)}, u32[]{:S(2)}) collective-permute-start(bf16[8,2048]{1,0:T(8,128)(2,1)S(1)} %slice.48), channel_id=1, source_target_pairs={{0,4},{4,8},{8,12},{12,16},{16,20},{20,24},{24,28},{1,5},{5,9},{9,... | collective-permute-start | bytes 98312 | tf_op jit(solution)/shard_map/ppermute | solution.py:523
  11.5 3.6 %conv_project.1 = (bf16[64,2048]{1,0:T(8,128)(2,1)}, f32[64,544]{1,0:T(8,128)}) custom-call(bf16[64,2048]{1,0:T(8,128)(2,1)} %x_ref.1, bf16[8,2048]{1,0:T(8,128)(2,1)} %copy-done.17, f32[4,2048]{1,0:T(4,128)} %weight_ref.4, f32[1,2048]{1,0:T(1,128)} %bitcast.80, bf16[544,2048]{1,0:T(8,128)(2,1)} %bitcast.76), custom_call_target="tpu_custom_call" | custom-call | tf_op jit(solution)/shard_map/conv_project/pallas_call | solution.py:64
  16.9 2.2 %collective-permute-start.4 = (bf16[640,512]{1,0:T(8,128)(2,1)}, bf16[640,512]{1,0:T(8,128)(2,1)S(1)}, u32[]{:S(2)}, u32[]{:S(2)}) collective-permute-start(bf16[640,512]{1,0:T(8,128)(2,1)} %slice.49), channel_id=1, source_target_pairs={{4,0},{0,4},{12,8},{8,12},{20,16},{16,20},{28,24},{24,28},{5,1},{1... | collective-permute-start | bytes 1966088 | tf_op jit(solution)/shard_map/ppermute | solution.py:482
  21.9 2.4 %collective-permute-done.3.refs_1_ = f32[64,544]{1,0:T(8,128)S(1)} collective-permute-done((f32[64,544]{1,0:T(8,128)S(1)}, f32[64,544]{1,0:T(8,128)S(1)}, u32[]{:S(2)}, u32[]{:S(2)}) %collective-permute-start.3) | collective-permute-done | bytes 139296 | tf_op jit(solution)/shard_map/ppermute | solution.py:514
  25.0 4.8 %scan_ends.1 = (f32[64,2048]{1,0:T(8,128)}, bf16[24,2048]{1,0:T(8,128)(2,1)}, f32[64,32]{1,0:T(8,128)}) custom-call(f32[64,544]{1,0:T(8,128)} %copy-done.7, f32[64,544]{1,0:T(8,128)} %copy-done.11, bf16[512,2048]{1,0:T(8,128)(2,1)} %refs_2_.1, f32[1,2048]{1,0:T(1,128)} %bitcast.81, f32[16,2048]{1,0:T(8,128)} %multiply_bitcast_fusion.refs_4_.refs_12_, ...), custom_call_target="tpu_custom_call" | custom-call | tf_op jit(solution)/shard_map/scan_ends/pallas_call | solution.py:145
  29.9 4.3 %collective-permute-done.4.refs_5_ = bf16[640,512]{1,0:T(8,128)(2,1)S(1)} collective-permute-done((bf16[640,512]{1,0:T(8,128)(2,1)}, bf16[640,512]{1,0:T(8,128)(2,1)S(1)}, u32[]{:S(2)}, u32[]{:S(2)}) %collective-permute-start.4) | collective-permute-done | bytes 655392 | tf_op jit(solution)/shard_map/ppermute | solution.py:482
  35.6 2.5 %collective-permute-start.6 = (bf16[24,2048]{1,0:T(8,128)(2,1)}, bf16[24,2048]{1,0:T(8,128)(2,1)S(1)}, u32[]{:S(2)}, u32[]{:S(2)}) collective-permute-start(bf16[24,2048]{1,0:T(8,128)(2,1)} %get-tuple-element.43.refs_0_), channel_id=1, source_target_pairs={{16,0},{20,4},{24,8},{28,12},{0,16},{4,20},{8,24},{12,28},{17,1},{... | collective-permute-start | bytes 294920 | tf_op jit(solution)/shard_map/ppermute | solution.py:474
  38.1 2.4 %collective-permute-start.5 = (bf16[24,2048]{1,0:T(8,128)(2,1)}, bf16[24,2048]{1,0:T(8,128)(2,1)S(1)}, u32[]{:S(2)}, u32[]{:S(2)}) collective-permute-start(bf16[24,2048]{1,0:T(8,128)(2,1)} %get-tuple-element.43.refs_0_), channel_id=1, source_target_pairs={{8,0},{12,4},{16,8},{20,12},{24,16},{28,20},{0,24},{4,28},{9,1},{1... | collective-permute-start | bytes 294920 | tf_op jit(solution)/shard_map/ppermute | solution.py:474
  41.7 2.6 %collective-permute-done.5.refs_2_ = bf16[24,2048]{1,0:T(8,128)(2,1)S(1)} collective-permute-done((bf16[24,2048]{1,0:T(8,128)(2,1)}, bf16[24,2048]{1,0:T(8,128)(2,1)S(1)}, u32[]{:S(2)}, u32[]{:S(2)}) %collective-permute-start.5) | collective-permute-done | bytes 98336 | tf_op jit(solution)/shard_map/ppermute | solution.py:474
  45.8 2.7 %collective-permute-done.9.refs_3_ = bf16[24,2048]{1,0:T(8,128)(2,1)S(1)} collective-permute-done((bf16[24,2048]{1,0:T(8,128)(2,1)S(1)}, bf16[24,2048]{1,0:T(8,128)(2,1)S(1)}, u32[]{:S(2)}, u32[]{:S(2)}) %collective-permute-start.9) | collective-permute-done | bytes 98336 | tf_op jit(solution)/shard_map/ppermute | solution.py:482
  51.1 2.9 %collective-permute-done.11.refs_5_ = bf16[24,2048]{1,0:T(8,128)(2,1)} collective-permute-done((bf16[24,2048]{1,0:T(8,128)(2,1)S(1)}, bf16[24,2048]{1,0:T(8,128)(2,1)}, u32[]{:S(2)}, u32[]{:S(2)}) %collective-permute-start.11) | collective-permute-done | bytes 98336 | tf_op jit(solution)/shard_map/ppermute | solution.py:482
  56.0 5.8 %scan_mix.1.refs_0_ = bf16[64,2048]{1,0:T(8,128)(2,1)} custom-call(s32[1]{0:T(128)} %bitcast.15.z_place.z_ref, s32[1]{0:T(128)} %bitcast.16.x_place.x_ref, bf16[24,2048]{1,0:T(8,128)(2,1)} %get-tuple-element.43.refs_0_, bf16[24,2048]{1,0:T(8,128)(2,1)} %collective-permute-done.8.refs_1_, bf16[24,2048]{1,0:T(8,128)(2,1)} %copy-done.10, ...), custom_call_target="tpu_custom_call" | custom-call | tf_op jit(solution)/shard_map/scan_mix/pallas_call | solution.py:241
  63.7 3.1 %collective-permute-start.13 = (bf16[64,2048]{1,0:T(8,128)(2,1)}, bf16[64,2048]{1,0:T(8,128)(2,1)}, u32[]{:S(2)}, u32[]{:S(2)}) collective-permute-start(bf16[64,2048]{1,0:T(8,128)(2,1)} %scan_mix.1.refs_0_), channel_id=1, source_target_pairs={{16,0},{20,4},{24,8},{28,12},{0,16},{4,20},{8,24},{12,28},{17,1},{... | collective-permute-start | bytes 786440 | tf_op jit(solution)/shard_map/ppermute | solution.py:474
  76.8 11.8 %collective-permute-done.13.refs_2_ = bf16[64,2048]{1,0:T(8,128)(2,1)} collective-permute-done((bf16[64,2048]{1,0:T(8,128)(2,1)}, bf16[64,2048]{1,0:T(8,128)(2,1)}, u32[]{:S(2)}, u32[]{:S(2)}) %collective-permute-start.13) | collective-permute-done | bytes 262176 | tf_op jit(solution)/shard_map/ppermute | solution.py:474
  91.5 3.1 %out_product.1 = (bf16[272,1024]{1,0:T(8,128)(2,1)S(1)}, bf16[272,1024]{1,0:T(8,128)(2,1)S(1)}) custom-call(s32[1]{0:T(128)} %bitcast.15.z_place.z_ref, s32[1]{0:T(128)} %bitcast.16.x_place.x_ref, s32[1]{0:T(128)} %bitcast.27.e_ref, bf16[272,256]{1,0:T(8,128)(2,1)S(1)} %get-tuple-element.66.keep_pick_ref, ...), custom_call_target="tpu_custom_call" | custom-call | tf_op jit(solution)/shard_map/out_product/pallas_call | solution.py:303
  94.6 2.7 %collective-permute-start.16 = (bf16[272,1024]{1,0:T(8,128)(2,1)S(1)}, bf16[272,1024]{1,0:T(8,128)(2,1)S(1)}, u32[]{:S(2)}, u32[]{:S(2)}) collective-permute-start(bf16[272,1024]{1,0:T(8,128)(2,1)S(1)} %get-tuple-element.51), channel_id=1, source_target_pairs={{1,0},{0,1},{3,2},{2,3},{5,4},{4,5},{7,6},{6,7},{9,8},{8,9},{11,10... | collective-permute-start | bytes 1671176 | tf_op jit(solution)/shard_map/ppermute | solution.py:506
  99.3 7.9 %collective-permute-done.17 = bf16[136,1024]{1,0:T(8,128)(2,1)S(1)} collective-permute-done((bf16[136,1024]{1,0:T(8,128)(2,1)S(1)}, bf16[136,1024]{1,0:T(8,128)(2,1)S(1)}, u32[]{:S(2)}, u32[]{:S(2)}) %collective-permute-start.17) | collective-permute-done | bytes 278560 | tf_op jit(solution)/shard_map/ppermute | solution.py:514
  109.8 4.5 %collective-permute-done.19.refs_2_ = bf16[136,1024]{1,0:T(8,128)(2,1)S(1)} collective-permute-done((bf16[136,1024]{1,0:T(8,128)(2,1)S(1)}, bf16[136,1024]{1,0:T(8,128)(2,1)S(1)}, u32[]{:S(2)}, u32[]{:S(2)}) %collective-permute-start.19) | collective-permute-done | bytes 278560 | tf_op jit(solution)/shard_map/ppermute | solution.py:474
  116.6 3.9 %collective-permute-done.22.refs_6_ = bf16[136,1024]{1,0:T(8,128)(2,1)S(1)} collective-permute-done((bf16[136,1024]{1,0:T(8,128)(2,1)S(1)}, bf16[136,1024]{1,0:T(8,128)(2,1)S(1)}, u32[]{:S(2)}, u32[]{:S(2)}) %collective-permute-start.22) | collective-permute-done | bytes 278560 | tf_op jit(solution)/shard_map/ppermute | solution.py:474
  121.0 8.4 %collective-permute-done.21.refs_4_ = bf16[136,1024]{1,0:T(8,128)(2,1)S(1)} collective-permute-done((bf16[136,1024]{1,0:T(8,128)(2,1)S(1)}, bf16[136,1024]{1,0:T(8,128)(2,1)S(1)}, u32[]{:S(2)}, u32[]{:S(2)}) %collective-permute-start.21) | collective-permute-done | bytes 278560 | tf_op jit(solution)/shard_map/ppermute | solution.py:474
  129.4 7.0 %collective-permute-done.24.refs_5_ = bf16[136,1024]{1,0:T(8,128)(2,1)S(1)} collective-permute-done((bf16[136,1024]{1,0:T(8,128)(2,1)S(1)}, bf16[136,1024]{1,0:T(8,128)(2,1)S(1)}, u32[]{:S(2)}, u32[]{:S(2)}) %collective-permute-start.24) | collective-permute-done | bytes 278560 | tf_op jit(solution)/shard_map/ppermute | solution.py:482
  136.4 13.9 %expert_hidden.1.act_ref = bf16[288,1536]{1,0:T(8,128)(2,1)S(1)} custom-call(s32[1]{0:T(128)} %bitcast.15.z_place.z_ref, s32[1]{0:T(128)} %bitcast.16.x_place.x_ref, bf16[136,1024]{1,0:T(8,128)(2,1)S(1)} %fusion.4.refs_0_, bf16[136,1024]{1,0:T(8,128)(2,1)S(1)} %collective-permute-done.18.refs_1_, bf16[136,1024]{1,0:T(8,128)(2,1)S(1)} %collective-permute-done.19.refs_2_, ...), custom_call_target="tpu_custom_call" | custom-call | tf_op jit(solution)/shard_map/expert_hidden/pallas_call | solution.py:371
  150.3 2.9 %expert_down.5 = (bf16[136,1024]{1,0:T(8,128)(2,1)S(1)}, bf16[136,1024]{1,0:T(8,128)(2,1)S(1)}) custom-call(s32[1]{0:T(128)} %bitcast.16.x_place.x_ref, s32[1]{0:T(128)} %bitcast.31.blocks_ref, bf16[288,1536]{1,0:T(8,128)(2,1)S(1)} %expert_hidden.1.act_ref, bf16[1,1536,4096]{2,1,0:T(8,128)(2,1)} %weight_ref.7), custom_call_target="tpu_custom_call" | custom-call | tf_op jit(solution)/shard_map/expert_down/pallas_call | solution.py:412
  154.3 5.7 %expert_down.3 = (bf16[136,1024]{1,0:T(8,128)(2,1)S(1)}, bf16[136,1024]{1,0:T(8,128)(2,1)S(1)}, bf16[136,1024]{1,0:T(8,128)(2,1)S(1)}, bf16[136,1024]{1,0:T(8,128)(2,1)S(1)}) custom-call(s32[1]{0:T(128)} %bitcast.16.x_place.x_ref, s32[2]{0:T(128)S(1)} %pad_add_fusion.blocks_ref, bf16[288,1536]{1,0:T(8,128)(2,1)S(1)} %expert_hidden.1.act_ref, ...), custom_call_target="tpu_custom_call" | custom-call | tf_op jit(solution)/shard_map/expert_down/pallas_call | solution.py:412
  161.6 2.1 %collective-permute-start.27 = (bf16[136,1024]{1,0:T(8,128)(2,1)S(1)}, bf16[136,1024]{1,0:T(8,128)(2,1)S(1)}, u32[]{:S(2)}, u32[]{:S(2)}) collective-permute-start(bf16[136,1024]{1,0:T(8,128)(2,1)S(1)} %add_convert_fusion.4), channel_id=1, source_target_pairs={{16,0},{20,4},{24,8},{28,12},{0,16},{4,20},{8,24},{12,28},{17,1},{... | collective-permute-start | bytes 835592 | tf_op jit(solution)/shard_map/ppermute | solution.py:474
  163.7 4.6 %collective-permute-done.25 = bf16[136,1024]{1,0:T(8,128)(2,1)S(1)} collective-permute-done((bf16[136,1024]{1,0:T(8,128)(2,1)S(1)}, bf16[136,1024]{1,0:T(8,128)(2,1)S(1)}, u32[]{:S(2)}, u32[]{:S(2)}) %collective-permute-start.25) | collective-permute-done | bytes 278560 | tf_op jit(solution)/shard_map/ppermute | solution.py:482
  168.4 2.9 %expert_down.4 = (bf16[136,1024]{1,0:T(8,128)(2,1)S(1)}, bf16[136,1024]{1,0:T(8,128)(2,1)S(1)}) custom-call(s32[1]{0:T(128)} %bitcast.16.x_place.x_ref, s32[1]{0:T(128)} %bitcast.26.blocks_ref, bf16[288,1536]{1,0:T(8,128)(2,1)S(1)} %expert_hidden.1.act_ref, bf16[1,1536,4096]{2,1,0:T(8,128)(2,1)} %weight_ref.7), custom_call_target="tpu_custom_call" | custom-call | tf_op jit(solution)/shard_map/expert_down/pallas_call | solution.py:412
  176.0 5.2 %collective-permute-done.31 = bf16[136,1024]{1,0:T(8,128)(2,1)S(1)} collective-permute-done((bf16[136,1024]{1,0:T(8,128)(2,1)S(1)}, bf16[136,1024]{1,0:T(8,128)(2,1)S(1)}, u32[]{:S(2)}, u32[]{:S(2)}) %collective-permute-start.31) | collective-permute-done | bytes 278560 | tf_op jit(solution)/shard_map/ppermute | solution.py:474
  181.6 13.8 %collective-permute-start.35 = (bf16[34,1024]{1,0:T(8,128)(2,1)S(1)}, bf16[34,1024]{1,0:T(8,128)(2,1)S(1)}, u32[]{:S(2)}, u32[]{:S(2)}) collective-permute-start(bf16[34,1024]{1,0:T(8,128)(2,1)S(1)} %get-tuple-element.68), channel_id=1, source_target_pairs={{3,0},{11,1},{19,2},{27,3},{7,4},{15,5},{23,6},{31,7},{0,8},{8,9},... | collective-permute-start | bytes 208904 | tf_op jit(solution)/shard_map/ppermute | solution.py:660
  196.3 6.2 %collective-permute-start.32 = (bf16[34,1024]{1,0:T(8,128)(2,1)S(1)}, bf16[34,1024]{1,0:T(8,128)(2,1)S(1)}, u32[]{:S(2)}, u32[]{:S(2)}) collective-permute-start(bf16[34,1024]{1,0:T(8,128)(2,1)S(1)} %get-tuple-element.67), channel_id=1, source_target_pairs={{0,0},{8,1},{16,2},{24,3},{4,4},{12,5},{20,6},{28,7},{1,8},{9,9},{... | collective-permute-start | bytes 208904 | tf_op jit(solution)/shard_map/ppermute | solution.py:660
  202.7 2.1 %collective-permute-done.32 = bf16[34,1024]{1,0:T(8,128)(2,1)S(1)} collective-permute-done((bf16[34,1024]{1,0:T(8,128)(2,1)S(1)}, bf16[34,1024]{1,0:T(8,128)(2,1)S(1)}, u32[]{:S(2)}, u32[]{:S(2)}) %collective-permute-start.32) | collective-permute-done | bytes 69664 | tf_op jit(solution)/shard_map/ppermute | solution.py:660
  (153 shorter events, 48.2 us)
Async XLA Ops:
  0.0 15.1 %collective-permute-start.1 = (bf16[64,1024]{1,0:T(8,128)(2,1)}, bf16[64,1024]{1,0:T(8,128)(2,1)S(1)}, u32[]{:S(2)}, u32[]{:S(2)}) collective-permute-start(bf16[64,1024]{1,0:T(8,128)(2,1)} %param.27), channel_id=1, source_target_pairs={{0,0},{8,1},{16,2},{24,3},{4,4},{12,5},{20,6},{28,7},{1,8},{9,9},{... | collective-permute-start | bytes 393224 | tf_op jit(solution)/shard_map/ppermute | solution.py:528
  16.9 17.3 %collective-permute-start.4 = (bf16[640,512]{1,0:T(8,128)(2,1)}, bf16[640,512]{1,0:T(8,128)(2,1)S(1)}, u32[]{:S(2)}, u32[]{:S(2)}) collective-permute-start(bf16[640,512]{1,0:T(8,128)(2,1)} %slice.49), channel_id=1, source_target_pairs={{4,0},{0,4},{12,8},{8,12},{20,16},{16,20},{28,24},{24,28},{5,1},{1... | collective-permute-start | bytes 1966088 | tf_op jit(solution)/shard_map/ppermute | solution.py:482
  19.1 5.3 %collective-permute-start.3 = (f32[64,544]{1,0:T(8,128)S(1)}, f32[64,544]{1,0:T(8,128)S(1)}, u32[]{:S(2)}, u32[]{:S(2)}) collective-permute-start(f32[64,544]{1,0:T(8,128)S(1)} %add.242.refs_0_), channel_id=1, source_target_pairs={{2,0},{3,1},{0,2},{1,3},{6,4},{7,5},{4,6},{5,7},{10,8},{11,9},{8,1... | collective-permute-start | bytes 417800 | tf_op jit(solution)/shard_map/ppermute | solution.py:514
  35.0 10.1 %collective-permute-start.7 = (bf16[24,2048]{1,0:T(8,128)(2,1)}, bf16[24,2048]{1,0:T(8,128)(2,1)S(1)}, u32[]{:S(2)}, u32[]{:S(2)}) collective-permute-start(bf16[24,2048]{1,0:T(8,128)(2,1)} %get-tuple-element.43.refs_0_), channel_id=1, source_target_pairs={{24,0},{28,4},{0,8},{4,12},{8,16},{12,20},{16,24},{20,28},{25,1},{... | collective-permute-start | bytes 294920 | tf_op jit(solution)/shard_map/ppermute | solution.py:474
  35.6 10.2 %collective-permute-start.6 = (bf16[24,2048]{1,0:T(8,128)(2,1)}, bf16[24,2048]{1,0:T(8,128)(2,1)S(1)}, u32[]{:S(2)}, u32[]{:S(2)}) collective-permute-start(bf16[24,2048]{1,0:T(8,128)(2,1)} %get-tuple-element.43.refs_0_), channel_id=1, source_target_pairs={{16,0},{20,4},{24,8},{28,12},{0,16},{4,20},{8,24},{12,28},{17,1},{... | collective-permute-start | bytes 294920 | tf_op jit(solution)/shard_map/ppermute | solution.py:474
  38.1 6.1 %collective-permute-start.5 = (bf16[24,2048]{1,0:T(8,128)(2,1)}, bf16[24,2048]{1,0:T(8,128)(2,1)S(1)}, u32[]{:S(2)}, u32[]{:S(2)}) collective-permute-start(bf16[24,2048]{1,0:T(8,128)(2,1)} %get-tuple-element.43.refs_0_), channel_id=1, source_target_pairs={{8,0},{12,4},{16,8},{20,12},{24,16},{28,20},{0,24},{4,28},{9,1},{1... | collective-permute-start | bytes 294920 | tf_op jit(solution)/shard_map/ppermute | solution.py:474
  41.3 9.3 %collective-permute-start.8 = (bf16[24,2048]{1,0:T(8,128)(2,1)}, bf16[24,2048]{1,0:T(8,128)(2,1)}, u32[]{:S(2)}, u32[]{:S(2)}) collective-permute-start(bf16[24,2048]{1,0:T(8,128)(2,1)} %get-tuple-element.43.refs_0_), channel_id=1, source_target_pairs={{4,0},{0,4},{12,8},{8,12},{20,16},{16,20},{28,24},{24,28},{5,1},{1... | collective-permute-start | bytes 294920 | tf_op jit(solution)/shard_map/ppermute | solution.py:482
  45.1 5.4 %collective-permute-start.10 = (bf16[24,2048]{1,0:T(8,128)(2,1)S(1)}, bf16[24,2048]{1,0:T(8,128)(2,1)S(1)}, u32[]{:S(2)}, u32[]{:S(2)}) collective-permute-start(bf16[24,2048]{1,0:T(8,128)(2,1)S(1)} %collective-permute-done.7.refs_6_), channel_id=1, source_target_pairs={{4,0},{0,4},{12,8},{8,12},{20,16},{16,20},{28,24},{24,28},{5,1},{1... | collective-permute-start | bytes 294920 | tf_op jit(solution)/shard_map/ppermute | solution.py:482
  55.3 33.3 %collective-permute-start.15 = (bf16[1408,512]{1,0:T(8,128)(2,1)}, bf16[1408,512]{1,0:T(8,128)(2,1)S(1)}, u32[]{:S(2)}, u32[]{:S(2)}) collective-permute-start(bf16[1408,512]{1,0:T(8,128)(2,1)} %slice.59), channel_id=1, source_target_pairs={{4,0},{0,4},{12,8},{8,12},{20,16},{16,20},{28,24},{24,28},{5,1},{1... | collective-permute-start | bytes 4325384 | tf_op jit(solution)/shard_map/ppermute | solution.py:482
  61.8 15.0 %collective-permute-start.12 = (bf16[64,2048]{1,0:T(8,128)(2,1)}, bf16[64,2048]{1,0:T(8,128)(2,1)}, u32[]{:S(2)}, u32[]{:S(2)}) collective-permute-start(bf16[64,2048]{1,0:T(8,128)(2,1)} %scan_mix.1.refs_0_), channel_id=1, source_target_pairs={{8,0},{12,4},{16,8},{20,12},{24,16},{28,20},{0,24},{4,28},{9,1},{1... | collective-permute-start | bytes 786440 | tf_op jit(solution)/shard_map/ppermute | solution.py:474
  63.7 24.9 %collective-permute-start.13 = (bf16[64,2048]{1,0:T(8,128)(2,1)}, bf16[64,2048]{1,0:T(8,128)(2,1)}, u32[]{:S(2)}, u32[]{:S(2)}) collective-permute-start(bf16[64,2048]{1,0:T(8,128)(2,1)} %scan_mix.1.refs_0_), channel_id=1, source_target_pairs={{16,0},{20,4},{24,8},{28,12},{0,16},{4,20},{8,24},{12,28},{17,1},{... | collective-permute-start | bytes 786440 | tf_op jit(solution)/shard_map/ppermute | solution.py:474
  66.8 21.8 %collective-permute-start.14 = (bf16[64,2048]{1,0:T(8,128)(2,1)}, bf16[64,2048]{1,0:T(8,128)(2,1)}, u32[]{:S(2)}, u32[]{:S(2)}) collective-permute-start(bf16[64,2048]{1,0:T(8,128)(2,1)} %scan_mix.1.refs_0_), channel_id=1, source_target_pairs={{24,0},{28,4},{0,8},{4,12},{8,16},{12,20},{16,24},{20,28},{25,1},{... | collective-permute-start | bytes 786440 | tf_op jit(solution)/shard_map/ppermute | solution.py:474
  94.6 4.3 %collective-permute-start.16 = (bf16[272,1024]{1,0:T(8,128)(2,1)S(1)}, bf16[272,1024]{1,0:T(8,128)(2,1)S(1)}, u32[]{:S(2)}, u32[]{:S(2)}) collective-permute-start(bf16[272,1024]{1,0:T(8,128)(2,1)S(1)} %get-tuple-element.51), channel_id=1, source_target_pairs={{1,0},{0,1},{3,2},{2,3},{5,4},{4,5},{7,6},{6,7},{9,8},{8,9},{11,10... | collective-permute-start | bytes 1671176 | tf_op jit(solution)/shard_map/ppermute | solution.py:506
  99.2 7.9 %collective-permute-start.17 = (bf16[136,1024]{1,0:T(8,128)(2,1)S(1)}, bf16[136,1024]{1,0:T(8,128)(2,1)S(1)}, u32[]{:S(2)}, u32[]{:S(2)}) collective-permute-start(bf16[136,1024]{1,0:T(8,128)(2,1)S(1)} %slice.92), channel_id=1, source_target_pairs={{2,0},{3,1},{0,2},{1,3},{6,4},{7,5},{4,6},{5,7},{10,8},{11,9},{8,1... | collective-permute-start | bytes 835592 | tf_op jit(solution)/shard_map/ppermute | solution.py:514
  107.2 7.1 %collective-permute-start.19 = (bf16[136,1024]{1,0:T(8,128)(2,1)S(1)}, bf16[136,1024]{1,0:T(8,128)(2,1)S(1)}, u32[]{:S(2)}, u32[]{:S(2)}) collective-permute-start(bf16[136,1024]{1,0:T(8,128)(2,1)S(1)} %fusion.4.refs_0_), channel_id=1, source_target_pairs={{8,0},{12,4},{16,8},{20,12},{24,16},{28,20},{0,24},{4,28},{9,1},{1... | collective-permute-start | bytes 835592 | tf_op jit(solution)/shard_map/ppermute | solution.py:474
  107.3 8.2 %collective-permute-start.18 = (bf16[136,1024]{1,0:T(8,128)(2,1)S(1)}, bf16[136,1024]{1,0:T(8,128)(2,1)S(1)}, u32[]{:S(2)}, u32[]{:S(2)}) collective-permute-start(bf16[136,1024]{1,0:T(8,128)(2,1)S(1)} %fusion.4.refs_0_), channel_id=1, source_target_pairs={{4,0},{0,4},{12,8},{8,12},{20,16},{16,20},{28,24},{24,28},{5,1},{1... | collective-permute-start | bytes 835592 | tf_op jit(solution)/shard_map/ppermute | solution.py:482
  108.4 12.2 %collective-permute-start.22 = (bf16[136,1024]{1,0:T(8,128)(2,1)S(1)}, bf16[136,1024]{1,0:T(8,128)(2,1)S(1)}, u32[]{:S(2)}, u32[]{:S(2)}) collective-permute-start(bf16[136,1024]{1,0:T(8,128)(2,1)S(1)} %fusion.4.refs_0_), channel_id=1, source_target_pairs={{24,0},{28,4},{0,8},{4,12},{8,16},{12,20},{16,24},{20,28},{25,1},{... | collective-permute-start | bytes 835592 | tf_op jit(solution)/shard_map/ppermute | solution.py:474
  114.3 6.7 %collective-permute-start.20 = (bf16[136,1024]{1,0:T(8,128)(2,1)S(1)}, bf16[136,1024]{1,0:T(8,128)(2,1)S(1)}, u32[]{:S(2)}, u32[]{:S(2)}) collective-permute-start(bf16[136,1024]{1,0:T(8,128)(2,1)S(1)} %collective-permute-done.19.refs_2_), channel_id=1, source_target_pairs={{4,0},{0,4},{12,8},{8,12},{20,16},{16,20},{28,24},{24,28},{5,1},{1... | collective-permute-start | bytes 835592 | tf_op jit(solution)/shard_map/ppermute | solution.py:482
  115.5 13.9 %collective-permute-start.21 = (bf16[136,1024]{1,0:T(8,128)(2,1)S(1)}, bf16[136,1024]{1,0:T(8,128)(2,1)S(1)}, u32[]{:S(2)}, u32[]{:S(2)}) collective-permute-start(bf16[136,1024]{1,0:T(8,128)(2,1)S(1)} %fusion.4.refs_0_), channel_id=1, source_target_pairs={{16,0},{20,4},{24,8},{28,12},{0,16},{4,20},{8,24},{12,28},{17,1},{... | collective-permute-start | bytes 835592 | tf_op jit(solution)/shard_map/ppermute | solution.py:474
  120.5 8.9 %collective-permute-start.23 = (bf16[136,1024]{1,0:T(8,128)(2,1)S(1)}, bf16[136,1024]{1,0:T(8,128)(2,1)S(1)}, u32[]{:S(2)}, u32[]{:S(2)}) collective-permute-start(bf16[136,1024]{1,0:T(8,128)(2,1)S(1)} %collective-permute-done.22.refs_6_), channel_id=1, source_target_pairs={{4,0},{0,4},{12,8},{8,12},{20,16},{16,20},{28,24},{24,28},{5,1},{1... | collective-permute-start | bytes 835592 | tf_op jit(solution)/shard_map/ppermute | solution.py:482
  129.4 7.0 %collective-permute-start.24 = (bf16[136,1024]{1,0:T(8,128)(2,1)S(1)}, bf16[136,1024]{1,0:T(8,128)(2,1)S(1)}, u32[]{:S(2)}, u32[]{:S(2)}) collective-permute-start(bf16[136,1024]{1,0:T(8,128)(2,1)S(1)} %collective-permute-done.21.refs_4_), channel_id=1, source_target_pairs={{4,0},{0,4},{12,8},{8,12},{20,16},{16,20},{28,24},{24,28},{5,1},{1... | collective-permute-start | bytes 835592 | tf_op jit(solution)/shard_map/ppermute | solution.py:482
  153.2 7.4 %collective-permute-start.26 = (bf16[136,1024]{1,0:T(8,128)(2,1)S(1)}, bf16[136,1024]{1,0:T(8,128)(2,1)S(1)}, u32[]{:S(2)}, u32[]{:S(2)}) collective-permute-start(bf16[136,1024]{1,0:T(8,128)(2,1)S(1)} %get-tuple-element.59), channel_id=1, source_target_pairs={{4,0},{0,4},{12,8},{8,12},{20,16},{16,20},{28,24},{24,28},{5,1},{1... | collective-permute-start | bytes 835592 | tf_op jit(solution)/shard_map/ppermute | solution.py:482
  160.0 8.3 %collective-permute-start.25 = (bf16[136,1024]{1,0:T(8,128)(2,1)S(1)}, bf16[136,1024]{1,0:T(8,128)(2,1)S(1)}, u32[]{:S(2)}, u32[]{:S(2)}) collective-permute-start(bf16[136,1024]{1,0:T(8,128)(2,1)S(1)} %get-tuple-element.54), channel_id=1, source_target_pairs={{4,0},{0,4},{12,8},{8,12},{20,16},{16,20},{28,24},{24,28},{5,1},{1... | collective-permute-start | bytes 835592 | tf_op jit(solution)/shard_map/ppermute | solution.py:482
  160.6 11.9 %collective-permute-start.30 = (bf16[136,1024]{1,0:T(8,128)(2,1)S(1)}, bf16[136,1024]{1,0:T(8,128)(2,1)S(1)}, u32[]{:S(2)}, u32[]{:S(2)}) collective-permute-start(bf16[136,1024]{1,0:T(8,128)(2,1)S(1)} %get-tuple-element.64), channel_id=1, source_target_pairs={{4,0},{0,4},{12,8},{8,12},{20,16},{16,20},{28,24},{24,28},{5,1},{1... | collective-permute-start | bytes 835592 | tf_op jit(solution)/shard_map/ppermute | solution.py:482
  161.6 13.1 %collective-permute-start.27 = (bf16[136,1024]{1,0:T(8,128)(2,1)S(1)}, bf16[136,1024]{1,0:T(8,128)(2,1)S(1)}, u32[]{:S(2)}, u32[]{:S(2)}) collective-permute-start(bf16[136,1024]{1,0:T(8,128)(2,1)S(1)} %add_convert_fusion.4), channel_id=1, source_target_pairs={{16,0},{20,4},{24,8},{28,12},{0,16},{4,20},{8,24},{12,28},{17,1},{... | collective-permute-start | bytes 835592 | tf_op jit(solution)/shard_map/ppermute | solution.py:474
  168.4 7.6 %collective-permute-start.29 = (bf16[136,1024]{1,0:T(8,128)(2,1)S(1)}, bf16[136,1024]{1,0:T(8,128)(2,1)S(1)}, u32[]{:S(2)}, u32[]{:S(2)}) collective-permute-start(bf16[136,1024]{1,0:T(8,128)(2,1)S(1)} %add_convert_fusion.3), channel_id=1, source_target_pairs={{24,0},{28,4},{0,8},{4,12},{8,16},{12,20},{16,24},{20,28},{25,1},{... | collective-permute-start | bytes 835592 | tf_op jit(solution)/shard_map/ppermute | solution.py:474
  172.6 8.6 %collective-permute-start.31 = (bf16[136,1024]{1,0:T(8,128)(2,1)S(1)}, bf16[136,1024]{1,0:T(8,128)(2,1)S(1)}, u32[]{:S(2)}, u32[]{:S(2)}) collective-permute-start(bf16[136,1024]{1,0:T(8,128)(2,1)S(1)} %add_convert_fusion.2), channel_id=1, source_target_pairs={{8,0},{12,4},{16,8},{20,12},{24,16},{28,20},{0,24},{4,28},{9,1},{1... | collective-permute-start | bytes 835592 | tf_op jit(solution)/shard_map/ppermute | solution.py:474
  174.7 6.5 %collective-permute-start.28 = (bf16[136,1024]{1,0:T(8,128)(2,1)S(1)}, bf16[136,1024]{1,0:T(8,128)(2,1)S(1)}, u32[]{:S(2)}, u32[]{:S(2)}) collective-permute-start(bf16[136,1024]{1,0:T(8,128)(2,1)S(1)} %get-tuple-element.60), channel_id=1, source_target_pairs={{4,0},{0,4},{12,8},{8,12},{20,16},{16,20},{28,24},{24,28},{5,1},{1... | collective-permute-start | bytes 835592 | tf_op jit(solution)/shard_map/ppermute | solution.py:482
  181.6 21.1 %collective-permute-start.35 = (bf16[34,1024]{1,0:T(8,128)(2,1)S(1)}, bf16[34,1024]{1,0:T(8,128)(2,1)S(1)}, u32[]{:S(2)}, u32[]{:S(2)}) collective-permute-start(bf16[34,1024]{1,0:T(8,128)(2,1)S(1)} %get-tuple-element.68), channel_id=1, source_target_pairs={{3,0},{11,1},{19,2},{27,3},{7,4},{15,5},{23,6},{31,7},{0,8},{8,9},... | collective-permute-start | bytes 208904 | tf_op jit(solution)/shard_map/ppermute | solution.py:660
  195.3 7.3 %collective-permute-start.34 = (bf16[34,1024]{1,0:T(8,128)(2,1)S(1)}, bf16[34,1024]{1,0:T(8,128)(2,1)S(1)}, u32[]{:S(2)}, u32[]{:S(2)}) collective-permute-start(bf16[34,1024]{1,0:T(8,128)(2,1)S(1)} %get-tuple-element.69), channel_id=1, source_target_pairs={{2,0},{10,1},{18,2},{26,3},{6,4},{14,5},{22,6},{30,7},{3,8},{11,9}... | collective-permute-start | bytes 208904 | tf_op jit(solution)/shard_map/ppermute | solution.py:660
  195.3 7.3 %collective-permute-start.33 = (bf16[34,1024]{1,0:T(8,128)(2,1)S(1)}, bf16[34,1024]{1,0:T(8,128)(2,1)S(1)}, u32[]{:S(2)}, u32[]{:S(2)}) collective-permute-start(bf16[34,1024]{1,0:T(8,128)(2,1)S(1)} %get-tuple-element.70), channel_id=1, source_target_pairs={{1,0},{9,1},{17,2},{25,3},{5,4},{13,5},{21,6},{29,7},{2,8},{10,9},... | collective-permute-start | bytes 208904 | tf_op jit(solution)/shard_map/ppermute | solution.py:660
  196.3 8.4 %collective-permute-start.32 = (bf16[34,1024]{1,0:T(8,128)(2,1)S(1)}, bf16[34,1024]{1,0:T(8,128)(2,1)S(1)}, u32[]{:S(2)}, u32[]{:S(2)}) collective-permute-start(bf16[34,1024]{1,0:T(8,128)(2,1)S(1)} %get-tuple-element.67), channel_id=1, source_target_pairs={{0,0},{8,1},{16,2},{24,3},{4,4},{12,5},{20,6},{28,7},{1,8},{9,9},{... | collective-permute-start | bytes 208904 | tf_op jit(solution)/shard_map/ppermute | solution.py:660
  (27 other events, 154.7 us)

commit v2 on v1

--- a/solution.py
+++ b/solution.py
@@ -483,14 +483,14 @@
 
     turns = sorted(range(1, z_count), key=lambda r: min(r, z_count - r))
 
-    def gathered(block, chained=True):
+    def gathered(block):
         rows = {(0, 0): block}
         others = range(1, x_count)
         for i in others:
             rows[0, i] = from_x(block, i)
         sent = block
         for k, r in enumerate(turns):
-            if chained and k >= 2:
+            if k >= 2:
                 sent = after(sent, rows[turns[k - 2], 0], *[rows[0, i] for i in others])
             rows[r, 0] = from_z(sent, r)
         for k, r in enumerate(turns):
@@ -561,7 +561,7 @@
     uppers = [from_x(after(out_proj, halo)[:cut], i) for i in range(1, x_count)]
     partials = [chip_sum] + [from_y(chip_sum, r) for r in range(1, y_count)]
     step_size, load, both = scan_ends(partials, dt_proj, dt_bias[None], rates, xconv, info)
-    loads = gathered(after(load, resid_here, *uppers), False)
+    loads = gathered(after(load, resid_here, *uppers))
     held_proj = after(out_proj, *[part for pair in loads for part in pair])
     lowers = [from_x(held_proj[cut:], i) for i in range(1, x_count)]
     columns = [[out_proj]] + [list(pair) for pair in zip(uppers, lowers)]

time: 208 us -> 208 us (level)
  starting transfers between devices: 59.6 us -> 38.6 us
  waiting for transfers between devices: 77 us -> 98 us
    ppermute x12, waiting for transfers between devices: 37.2 us -> 54.9 us  [from_z(): return lax.ppermute(block, 'seq', pairs)]
    ppermute x4, starting transfers between devices: 21 us -> 8.02 us  [per_device(): back.append(lax.ppermute(piece, ('seq', 'exp'), pairs))]
    ppermute x12, starting transfers between devices: 17.3 us -> 9.08 us  [from_z(): return lax.ppermute(block, 'seq', pairs)]
    ppermute x14, waiting for transfers between devices: 24.8 us -> 27.7 us  [from_x(): return lax.ppermute(block, 'seq', pairs)]
  transfers between devices with their start and end apart: 36 -> 36, of which waited for: 19 -> 21; matrix products, arithmetic and copies ran while one was open for 8% -> 8% of each run, Pallas kernels for 11% -> 11%
where the time goes in v2:
time: 208 us; the launch traced here: 206 us
  waiting for transfers between devices  98 us (47%)
  Pallas kernels  42.7 us (21%)
  starting transfers between devices  38.6 us (19%)
  local copies, waits for them, and re-layouts  17.1 us (8%)
  other arithmetic  6.72 us (3%)
    ppermute x12, waiting for transfers between devices, from_z(): return lax.ppermute(block, 'seq', pairs)  54.9 us
    ppermute x14, waiting for transfers between devices, from_x(): return lax.ppermute(block, 'seq', pairs)  27.7 us
    pallas_call x1, Pallas kernels, expert_hidden(): pl.pallas_call(functools.partial(hidden_kernel, z_count, x_count), grid=(...  13.9 us
    pallas_call x3, Pallas kernels, expert_down(): pl.pallas_call(functools.partial(down_kernel, x_count), grid_spec=pltpu.P...  11.4 us
    ppermute x2, waiting for transfers between devices, from_y(): return lax.ppermute(block, 'exp', pairs)  10.3 us
    ppermute x12, starting transfers between devices, from_z(): return lax.ppermute(block, 'seq', pairs)  9.08 us
    ppermute x14, starting transfers between devices, from_x(): return lax.ppermute(block, 'seq', pairs)  8.94 us
    ppermute x4, starting transfers between devices, per_device(): back.append(lax.ppermute(piece, ('seq', 'exp'), pairs))  8.02 us
  transfers between devices with their start and end apart: 36, of which 21 were waited for; matrix products, arithmetic and copies ran while one was open for 8% of the time, Pallas kernels for 11%

profile of v2, /device:TPU:5, one launch (start us, length us, event | category | flops | bytes accessed | tf_op | source)
XLA Modules:
  0.0 205.7 jit_solution(11043904643276810985)
XLA Ops:
  0.0 5.9 %collective-permute-start.1 = (bf16[64,1024]{1,0:T(8,128)(2,1)}, bf16[64,1024]{1,0:T(8,128)(2,1)S(1)}, u32[]{:S(2)}, u32[]{:S(2)}) collective-permute-start(bf16[64,1024]{1,0:T(8,128)(2,1)} %param.27), channel_id=1, source_target_pairs={{0,0},{8,1},{16,2},{24,3},{4,4},{12,5},{20,6},{28,7},{1,8},{9,9},{... | collective-permute-start | bytes 393224 | tf_op jit(solution)/shard_map/ppermute | solution.py:528
  6.6 3.1 %collective-permute-start = (bf16[8,2048]{1,0:T(8,128)(2,1)S(1)}, bf16[8,2048]{1,0:T(8,128)(2,1)S(1)}, u32[]{:S(2)}, u32[]{:S(2)}) collective-permute-start(bf16[8,2048]{1,0:T(8,128)(2,1)S(1)} %slice.48), channel_id=1, source_target_pairs={{0,4},{4,8},{8,12},{12,16},{16,20},{20,24},{24,28},{1,5},{5,9},{9,... | collective-permute-start | bytes 98312 | tf_op jit(solution)/shard_map/ppermute | solution.py:523
  11.5 3.6 %conv_project.1 = (bf16[64,2048]{1,0:T(8,128)(2,1)}, f32[64,544]{1,0:T(8,128)}) custom-call(bf16[64,2048]{1,0:T(8,128)(2,1)} %x_ref.1, bf16[8,2048]{1,0:T(8,128)(2,1)} %copy-done.17, f32[4,2048]{1,0:T(4,128)} %weight_ref.4, f32[1,2048]{1,0:T(1,128)} %bitcast.80, bf16[544,2048]{1,0:T(8,128)(2,1)} %bitcast.76), custom_call_target="tpu_custom_call" | custom-call | tf_op jit(solution)/shard_map/conv_project/pallas_call | solution.py:64
  16.9 2.2 %collective-permute-start.4 = (bf16[640,512]{1,0:T(8,128)(2,1)}, bf16[640,512]{1,0:T(8,128)(2,1)S(1)}, u32[]{:S(2)}, u32[]{:S(2)}) collective-permute-start(bf16[640,512]{1,0:T(8,128)(2,1)} %slice.49), channel_id=1, source_target_pairs={{4,0},{0,4},{12,8},{8,12},{20,16},{16,20},{28,24},{24,28},{5,1},{1... | collective-permute-start | bytes 1966088 | tf_op jit(solution)/shard_map/ppermute | solution.py:482
  21.9 2.4 %collective-permute-done.3.refs_1_ = f32[64,544]{1,0:T(8,128)S(1)} collective-permute-done((f32[64,544]{1,0:T(8,128)S(1)}, f32[64,544]{1,0:T(8,128)S(1)}, u32[]{:S(2)}, u32[]{:S(2)}) %collective-permute-start.3) | collective-permute-done | bytes 139296 | tf_op jit(solution)/shard_map/ppermute | solution.py:514
  25.0 4.8 %scan_ends.1 = (f32[64,2048]{1,0:T(8,128)}, bf16[24,2048]{1,0:T(8,128)(2,1)}, f32[64,32]{1,0:T(8,128)}) custom-call(f32[64,544]{1,0:T(8,128)} %copy-done.7, f32[64,544]{1,0:T(8,128)} %copy-done.11, bf16[512,2048]{1,0:T(8,128)(2,1)} %refs_2_.1, f32[1,2048]{1,0:T(1,128)} %bitcast.81, f32[16,2048]{1,0:T(8,128)} %multiply_bitcast_fusion.refs_4_.refs_12_, ...), custom_call_target="tpu_custom_call" | custom-call | tf_op jit(solution)/shard_map/scan_ends/pallas_call | solution.py:145
  29.9 4.3 %collective-permute-done.4.refs_5_ = bf16[640,512]{1,0:T(8,128)(2,1)S(1)} collective-permute-done((bf16[640,512]{1,0:T(8,128)(2,1)}, bf16[640,512]{1,0:T(8,128)(2,1)S(1)}, u32[]{:S(2)}, u32[]{:S(2)}) %collective-permute-start.4) | collective-permute-done | bytes 655392 | tf_op jit(solution)/shard_map/ppermute | solution.py:482
  35.6 2.7 %collective-permute-start.5 = (bf16[24,2048]{1,0:T(8,128)(2,1)}, bf16[24,2048]{1,0:T(8,128)(2,1)S(1)}, u32[]{:S(2)}, u32[]{:S(2)}) collective-permute-start(bf16[24,2048]{1,0:T(8,128)(2,1)} %get-tuple-element.45.refs_0_), channel_id=1, source_target_pairs={{8,0},{12,4},{16,8},{20,12},{24,16},{28,20},{0,24},{4,28},{9,1},{1... | collective-permute-start | bytes 294920 | tf_op jit(solution)/shard_map/ppermute | solution.py:474
  40.2 3.4 %collective-permute-done.5.refs_2_ = bf16[24,2048]{1,0:T(8,128)(2,1)S(1)} collective-permute-done((bf16[24,2048]{1,0:T(8,128)(2,1)}, bf16[24,2048]{1,0:T(8,128)(2,1)S(1)}, u32[]{:S(2)}, u32[]{:S(2)}) %collective-permute-start.5) | collective-permute-done | bytes 98336 | tf_op jit(solution)/shard_map/ppermute | solution.py:474
  45.2 5.5 %collective-permute-done.7.refs_4_ = bf16[24,2048]{1,0:T(8,128)(2,1)S(1)} collective-permute-done((bf16[24,2048]{1,0:T(8,128)(2,1)}, bf16[24,2048]{1,0:T(8,128)(2,1)S(1)}, u32[]{:S(2)}, u32[]{:S(2)}) %collective-permute-start.7) | collective-permute-done | bytes 98336 | tf_op jit(solution)/shard_map/ppermute | solution.py:474
  51.4 2.9 %collective-permute-done.11.refs_5_ = bf16[24,2048]{1,0:T(8,128)(2,1)} collective-permute-done((bf16[24,2048]{1,0:T(8,128)(2,1)S(1)}, bf16[24,2048]{1,0:T(8,128)(2,1)}, u32[]{:S(2)}, u32[]{:S(2)}) %collective-permute-start.11) | collective-permute-done | bytes 98336 | tf_op jit(solution)/shard_map/ppermute | solution.py:482
  56.3 5.8 %scan_mix.1.refs_0_ = bf16[64,2048]{1,0:T(8,128)(2,1)} custom-call(s32[1]{0:T(128)} %bitcast.15.z_place.z_ref, s32[1]{0:T(128)} %bitcast.16.x_place.x_ref, bf16[24,2048]{1,0:T(8,128)(2,1)} %get-tuple-element.45.refs_0_, bf16[24,2048]{1,0:T(8,128)(2,1)} %collective-permute-done.6.refs_1_, bf16[24,2048]{1,0:T(8,128)(2,1)} %copy-done.9, ...), custom_call_target="tpu_custom_call" | custom-call | tf_op jit(solution)/shard_map/scan_mix/pallas_call | solution.py:241
  74.2 9.0 %collective-permute-done.13.refs_2_ = bf16[64,2048]{1,0:T(8,128)(2,1)} collective-permute-done((bf16[64,2048]{1,0:T(8,128)(2,1)}, bf16[64,2048]{1,0:T(8,128)(2,1)}, u32[]{:S(2)}, u32[]{:S(2)}) %collective-permute-start.13) | collective-permute-done | bytes 262176 | tf_op jit(solution)/shard_map/ppermute | solution.py:474
  83.2 3.4 %collective-permute-done.15.refs_6_ = bf16[1408,512]{1,0:T(8,128)(2,1)S(1)} collective-permute-done((bf16[1408,512]{1,0:T(8,128)(2,1)}, bf16[1408,512]{1,0:T(8,128)(2,1)S(1)}, u32[]{:S(2)}, u32[]{:S(2)}) %collective-permute-start.15) | collective-permute-done | bytes 1441824 | tf_op jit(solution)/shard_map/ppermute | solution.py:482
  89.6 3.1 %out_product.1 = (bf16[272,1024]{1,0:T(8,128)(2,1)S(1)}, bf16[272,1024]{1,0:T(8,128)(2,1)S(1)}) custom-call(s32[1]{0:T(128)} %bitcast.15.z_place.z_ref, s32[1]{0:T(128)} %bitcast.16.x_place.x_ref, s32[1]{0:T(128)} %bitcast.27.e_ref, bf16[272,256]{1,0:T(8,128)(2,1)S(1)} %get-tuple-element.68.keep_pick_ref, ...), custom_call_target="tpu_custom_call" | custom-call | tf_op jit(solution)/shard_map/out_product/pallas_call | solution.py:303
  92.7 3.3 %collective-permute-start.16 = (bf16[272,1024]{1,0:T(8,128)(2,1)S(1)}, bf16[272,1024]{1,0:T(8,128)(2,1)S(1)}, u32[]{:S(2)}, u32[]{:S(2)}) collective-permute-start(bf16[272,1024]{1,0:T(8,128)(2,1)S(1)} %get-tuple-element.53), channel_id=1, source_target_pairs={{1,0},{0,1},{3,2},{2,3},{5,4},{4,5},{7,6},{6,7},{9,8},{8,9},{11,10... | collective-permute-start | bytes 1671176 | tf_op jit(solution)/shard_map/ppermute | solution.py:506
  97.8 7.9 %collective-permute-done.17 = bf16[136,1024]{1,0:T(8,128)(2,1)S(1)} collective-permute-done((bf16[136,1024]{1,0:T(8,128)(2,1)S(1)}, bf16[136,1024]{1,0:T(8,128)(2,1)S(1)}, u32[]{:S(2)}, u32[]{:S(2)}) %collective-permute-start.17) | collective-permute-done | bytes 278560 | tf_op jit(solution)/shard_map/ppermute | solution.py:514
  107.3 5.5 %collective-permute-done.19.refs_2_ = bf16[136,1024]{1,0:T(8,128)(2,1)S(1)} collective-permute-done((bf16[136,1024]{1,0:T(8,128)(2,1)S(1)}, bf16[136,1024]{1,0:T(8,128)(2,1)S(1)}, u32[]{:S(2)}, u32[]{:S(2)}) %collective-permute-start.19) | collective-permute-done | bytes 278560 | tf_op jit(solution)/shard_map/ppermute | solution.py:474
  113.5 5.4 %collective-permute-done.22.refs_6_ = bf16[136,1024]{1,0:T(8,128)(2,1)S(1)} collective-permute-done((bf16[136,1024]{1,0:T(8,128)(2,1)S(1)}, bf16[136,1024]{1,0:T(8,128)(2,1)S(1)}, u32[]{:S(2)}, u32[]{:S(2)}) %collective-permute-start.22) | collective-permute-done | bytes 278560 | tf_op jit(solution)/shard_map/ppermute | solution.py:474
  119.2 13.2 %collective-permute-done.21.refs_4_ = bf16[136,1024]{1,0:T(8,128)(2,1)S(1)} collective-permute-done((bf16[136,1024]{1,0:T(8,128)(2,1)S(1)}, bf16[136,1024]{1,0:T(8,128)(2,1)S(1)}, u32[]{:S(2)}, u32[]{:S(2)}) %collective-permute-start.21) | collective-permute-done | bytes 278560 | tf_op jit(solution)/shard_map/ppermute | solution.py:474
  132.8 7.4 %collective-permute-done.24.refs_5_ = bf16[136,1024]{1,0:T(8,128)(2,1)S(1)} collective-permute-done((bf16[136,1024]{1,0:T(8,128)(2,1)S(1)}, bf16[136,1024]{1,0:T(8,128)(2,1)S(1)}, u32[]{:S(2)}, u32[]{:S(2)}) %collective-permute-start.24) | collective-permute-done | bytes 278560 | tf_op jit(solution)/shard_map/ppermute | solution.py:482
  140.2 13.9 %expert_hidden.1.act_ref = bf16[288,1536]{1,0:T(8,128)(2,1)S(1)} custom-call(s32[1]{0:T(128)} %bitcast.15.z_place.z_ref, s32[1]{0:T(128)} %bitcast.16.x_place.x_ref, bf16[136,1024]{1,0:T(8,128)(2,1)S(1)} %fusion.4.refs_0_, bf16[136,1024]{1,0:T(8,128)(2,1)S(1)} %collective-permute-done.18.refs_1_, bf16[136,1024]{1,0:T(8,128)(2,1)S(1)} %collective-permute-done.19.refs_2_, ...), custom_call_target="tpu_custom_call" | custom-call | tf_op jit(solution)/shard_map/expert_hidden/pallas_call | solution.py:371
  154.1 2.9 %expert_down.5 = (bf16[136,1024]{1,0:T(8,128)(2,1)S(1)}, bf16[136,1024]{1,0:T(8,128)(2,1)S(1)}) custom-call(s32[1]{0:T(128)} %bitcast.16.x_place.x_ref, s32[1]{0:T(128)} %bitcast.31.blocks_ref, bf16[288,1536]{1,0:T(8,128)(2,1)S(1)} %expert_hidden.1.act_ref, bf16[1,1536,4096]{2,1,0:T(8,128)(2,1)} %weight_ref.7), custom_call_target="tpu_custom_call" | custom-call | tf_op jit(solution)/shard_map/expert_down/pallas_call | solution.py:412
  157.4 5.7 %expert_down.3 = (bf16[136,1024]{1,0:T(8,128)(2,1)S(1)}, bf16[136,1024]{1,0:T(8,128)(2,1)S(1)}, bf16[136,1024]{1,0:T(8,128)(2,1)S(1)}, bf16[136,1024]{1,0:T(8,128)(2,1)S(1)}) custom-call(s32[1]{0:T(128)} %bitcast.16.x_place.x_ref, s32[2]{0:T(128)S(1)} %pad_add_fusion.blocks_ref, bf16[288,1536]{1,0:T(8,128)(2,1)S(1)} %expert_hidden.1.act_ref, ...), custom_call_target="tpu_custom_call" | custom-call | tf_op jit(solution)/shard_map/expert_down/pallas_call | solution.py:412
  164.8 4.9 %collective-permute-done.25 = bf16[136,1024]{1,0:T(8,128)(2,1)S(1)} collective-permute-done((bf16[136,1024]{1,0:T(8,128)(2,1)S(1)}, bf16[136,1024]{1,0:T(8,128)(2,1)S(1)}, u32[]{:S(2)}, u32[]{:S(2)}) %collective-permute-start.25) | collective-permute-done | bytes 278560 | tf_op jit(solution)/shard_map/ppermute | solution.py:482
  169.8 2.9 %expert_down.4 = (bf16[136,1024]{1,0:T(8,128)(2,1)S(1)}, bf16[136,1024]{1,0:T(8,128)(2,1)S(1)}) custom-call(s32[1]{0:T(128)} %bitcast.16.x_place.x_ref, s32[1]{0:T(128)} %bitcast.26.blocks_ref, bf16[288,1536]{1,0:T(8,128)(2,1)S(1)} %expert_hidden.1.act_ref, bf16[1,1536,4096]{2,1,0:T(8,128)(2,1)} %weight_ref.7), custom_call_target="tpu_custom_call" | custom-call | tf_op jit(solution)/shard_map/expert_down/pallas_call | solution.py:412
  172.7 2.9 %collective-permute-done.30 = bf16[136,1024]{1,0:T(8,128)(2,1)S(1)} collective-permute-done((bf16[136,1024]{1,0:T(8,128)(2,1)S(1)}, bf16[136,1024]{1,0:T(8,128)(2,1)S(1)}, u32[]{:S(2)}, u32[]{:S(2)}) %collective-permute-start.30) | collective-permute-done | bytes 278560 | tf_op jit(solution)/shard_map/ppermute | solution.py:482
  175.7 2.3 %collective-permute-start.31 = (bf16[136,1024]{1,0:T(8,128)(2,1)S(1)}, bf16[136,1024]{1,0:T(8,128)(2,1)S(1)}, u32[]{:S(2)}, u32[]{:S(2)}) collective-permute-start(bf16[136,1024]{1,0:T(8,128)(2,1)S(1)} %add_convert_fusion.2), channel_id=1, source_target_pairs={{8,0},{12,4},{16,8},{20,12},{24,16},{28,20},{0,24},{4,28},{9,1},{1... | collective-permute-start | bytes 835592 | tf_op jit(solution)/shard_map/ppermute | solution.py:474
  178.1 8.1 %collective-permute-done.27 = bf16[136,1024]{1,0:T(8,128)(2,1)S(1)} collective-permute-done((bf16[136,1024]{1,0:T(8,128)(2,1)S(1)}, bf16[136,1024]{1,0:T(8,128)(2,1)S(1)}, u32[]{:S(2)}, u32[]{:S(2)}) %collective-permute-start.27) | collective-permute-done | bytes 278560 | tf_op jit(solution)/shard_map/ppermute | solution.py:474
  187.2 4.8 %collective-permute-done.31 = bf16[136,1024]{1,0:T(8,128)(2,1)S(1)} collective-permute-done((bf16[136,1024]{1,0:T(8,128)(2,1)S(1)}, bf16[136,1024]{1,0:T(8,128)(2,1)S(1)}, u32[]{:S(2)}, u32[]{:S(2)}) %collective-permute-start.31) | collective-permute-done | bytes 278560 | tf_op jit(solution)/shard_map/ppermute | solution.py:474
  196.3 5.8 %collective-permute-start.32 = (bf16[34,1024]{1,0:T(8,128)(2,1)S(1)}, bf16[34,1024]{1,0:T(8,128)(2,1)S(1)}, u32[]{:S(2)}, u32[]{:S(2)}) collective-permute-start(bf16[34,1024]{1,0:T(8,128)(2,1)S(1)} %get-tuple-element.69), channel_id=1, source_target_pairs={{0,0},{8,1},{16,2},{24,3},{4,4},{12,5},{20,6},{28,7},{1,8},{9,9},{... | collective-permute-start | bytes 208904 | tf_op jit(solution)/shard_map/ppermute | solution.py:660
  202.3 2.5 %collective-permute-done.32 = bf16[34,1024]{1,0:T(8,128)(2,1)S(1)} collective-permute-done((bf16[34,1024]{1,0:T(8,128)(2,1)S(1)}, bf16[34,1024]{1,0:T(8,128)(2,1)S(1)}, u32[]{:S(2)}, u32[]{:S(2)}) %collective-permute-start.32) | collective-permute-done | bytes 69664 | tf_op jit(solution)/shard_map/ppermute | solution.py:660
  (153 shorter events, 43.7 us)
Async XLA Ops:
  0.0 15.1 %collective-permute-start.1 = (bf16[64,1024]{1,0:T(8,128)(2,1)}, bf16[64,1024]{1,0:T(8,128)(2,1)S(1)}, u32[]{:S(2)}, u32[]{:S(2)}) collective-permute-start(bf16[64,1024]{1,0:T(8,128)(2,1)} %param.27), channel_id=1, source_target_pairs={{0,0},{8,1},{16,2},{24,3},{4,4},{12,5},{20,6},{28,7},{1,8},{9,9},{... | collective-permute-start | bytes 393224 | tf_op jit(solution)/shard_map/ppermute | solution.py:528
  16.9 17.3 %collective-permute-start.4 = (bf16[640,512]{1,0:T(8,128)(2,1)}, bf16[640,512]{1,0:T(8,128)(2,1)S(1)}, u32[]{:S(2)}, u32[]{:S(2)}) collective-permute-start(bf16[640,512]{1,0:T(8,128)(2,1)} %slice.49), channel_id=1, source_target_pairs={{4,0},{0,4},{12,8},{8,12},{20,16},{16,20},{28,24},{24,28},{5,1},{1... | collective-permute-start | bytes 1966088 | tf_op jit(solution)/shard_map/ppermute | solution.py:482
  19.1 5.3 %collective-permute-start.3 = (f32[64,544]{1,0:T(8,128)S(1)}, f32[64,544]{1,0:T(8,128)S(1)}, u32[]{:S(2)}, u32[]{:S(2)}) collective-permute-start(f32[64,544]{1,0:T(8,128)S(1)} %add.242.refs_0_), channel_id=1, source_target_pairs={{2,0},{3,1},{0,2},{1,3},{6,4},{7,5},{4,6},{5,7},{10,8},{11,9},{8,1... | collective-permute-start | bytes 417800 | tf_op jit(solution)/shard_map/ppermute | solution.py:514
  35.0 8.9 %collective-permute-start.8 = (bf16[24,2048]{1,0:T(8,128)(2,1)}, bf16[24,2048]{1,0:T(8,128)(2,1)S(1)}, u32[]{:S(2)}, u32[]{:S(2)}) collective-permute-start(bf16[24,2048]{1,0:T(8,128)(2,1)} %get-tuple-element.45.refs_0_), channel_id=1, source_target_pairs={{24,0},{28,4},{0,8},{4,12},{8,16},{12,20},{16,24},{20,28},{25,1},{... | collective-permute-start | bytes 294920 | tf_op jit(solution)/shard_map/ppermute | solution.py:474
  35.6 8.1 %collective-permute-start.5 = (bf16[24,2048]{1,0:T(8,128)(2,1)}, bf16[24,2048]{1,0:T(8,128)(2,1)S(1)}, u32[]{:S(2)}, u32[]{:S(2)}) collective-permute-start(bf16[24,2048]{1,0:T(8,128)(2,1)} %get-tuple-element.45.refs_0_), channel_id=1, source_target_pairs={{8,0},{12,4},{16,8},{20,12},{24,16},{28,20},{0,24},{4,28},{9,1},{1... | collective-permute-start | bytes 294920 | tf_op jit(solution)/shard_map/ppermute | solution.py:474
  38.3 5.3 %collective-permute-start.6 = (bf16[24,2048]{1,0:T(8,128)(2,1)}, bf16[24,2048]{1,0:T(8,128)(2,1)}, u32[]{:S(2)}, u32[]{:S(2)}) collective-permute-start(bf16[24,2048]{1,0:T(8,128)(2,1)} %get-tuple-element.45.refs_0_), channel_id=1, source_target_pairs={{4,0},{0,4},{12,8},{8,12},{20,16},{16,20},{28,24},{24,28},{5,1},{1... | collective-permute-start | bytes 294920 | tf_op jit(solution)/shard_map/ppermute | solution.py:482
  43.6 7.1 %collective-permute-start.7 = (bf16[24,2048]{1,0:T(8,128)(2,1)}, bf16[24,2048]{1,0:T(8,128)(2,1)S(1)}, u32[]{:S(2)}, u32[]{:S(2)}) collective-permute-start(bf16[24,2048]{1,0:T(8,128)(2,1)} %get-tuple-element.45.refs_0_), channel_id=1, source_target_pairs={{16,0},{20,4},{24,8},{28,12},{0,16},{4,20},{8,24},{12,28},{17,1},{... | collective-permute-start | bytes 294920 | tf_op jit(solution)/shard_map/ppermute | solution.py:474
  43.6 7.1 %collective-permute-start.9 = (bf16[24,2048]{1,0:T(8,128)(2,1)S(1)}, bf16[24,2048]{1,0:T(8,128)(2,1)S(1)}, u32[]{:S(2)}, u32[]{:S(2)}) collective-permute-start(bf16[24,2048]{1,0:T(8,128)(2,1)S(1)} %collective-permute-done.5.refs_2_), channel_id=1, source_target_pairs={{4,0},{0,4},{12,8},{8,12},{20,16},{16,20},{28,24},{24,28},{5,1},{1... | collective-permute-start | bytes 294920 | tf_op jit(solution)/shard_map/ppermute | solution.py:482
  43.9 6.8 %collective-permute-start.10 = (bf16[24,2048]{1,0:T(8,128)(2,1)S(1)}, bf16[24,2048]{1,0:T(8,128)(2,1)S(1)}, u32[]{:S(2)}, u32[]{:S(2)}) collective-permute-start(bf16[24,2048]{1,0:T(8,128)(2,1)S(1)} %collective-permute-done.8.refs_6_), channel_id=1, source_target_pairs={{4,0},{0,4},{12,8},{8,12},{20,16},{16,20},{28,24},{24,28},{5,1},{1... | collective-permute-start | bytes 294920 | tf_op jit(solution)/shard_map/ppermute | solution.py:482
  55.6 31.0 %collective-permute-start.15 = (bf16[1408,512]{1,0:T(8,128)(2,1)}, bf16[1408,512]{1,0:T(8,128)(2,1)S(1)}, u32[]{:S(2)}, u32[]{:S(2)}) collective-permute-start(bf16[1408,512]{1,0:T(8,128)(2,1)} %slice.59), channel_id=1, source_target_pairs={{4,0},{0,4},{12,8},{8,12},{20,16},{16,20},{28,24},{24,28},{5,1},{1... | collective-permute-start | bytes 4325384 | tf_op jit(solution)/shard_map/ppermute | solution.py:482
  62.1 12.1 %collective-permute-start.12 = (bf16[64,2048]{1,0:T(8,128)(2,1)}, bf16[64,2048]{1,0:T(8,128)(2,1)}, u32[]{:S(2)}, u32[]{:S(2)}) collective-permute-start(bf16[64,2048]{1,0:T(8,128)(2,1)} %scan_mix.1.refs_0_), channel_id=1, source_target_pairs={{8,0},{12,4},{16,8},{20,12},{24,16},{28,20},{0,24},{4,28},{9,1},{1... | collective-permute-start | bytes 786440 | tf_op jit(solution)/shard_map/ppermute | solution.py:474
  63.3 19.9 %collective-permute-start.13 = (bf16[64,2048]{1,0:T(8,128)(2,1)}, bf16[64,2048]{1,0:T(8,128)(2,1)}, u32[]{:S(2)}, u32[]{:S(2)}) collective-permute-start(bf16[64,2048]{1,0:T(8,128)(2,1)} %scan_mix.1.refs_0_), channel_id=1, source_target_pairs={{16,0},{20,4},{24,8},{28,12},{0,16},{4,20},{8,24},{12,28},{17,1},{... | collective-permute-start | bytes 786440 | tf_op jit(solution)/shard_map/ppermute | solution.py:474
  63.3 19.9 %collective-permute-start.14 = (bf16[64,2048]{1,0:T(8,128)(2,1)}, bf16[64,2048]{1,0:T(8,128)(2,1)}, u32[]{:S(2)}, u32[]{:S(2)}) collective-permute-start(bf16[64,2048]{1,0:T(8,128)(2,1)} %scan_mix.1.refs_0_), channel_id=1, source_target_pairs={{24,0},{28,4},{0,8},{4,12},{8,16},{12,20},{16,24},{20,28},{25,1},{... | collective-permute-start | bytes 786440 | tf_op jit(solution)/shard_map/ppermute | solution.py:474
  97.8 7.9 %collective-permute-start.17 = (bf16[136,1024]{1,0:T(8,128)(2,1)S(1)}, bf16[136,1024]{1,0:T(8,128)(2,1)S(1)}, u32[]{:S(2)}, u32[]{:S(2)}) collective-permute-start(bf16[136,1024]{1,0:T(8,128)(2,1)S(1)} %slice.92), channel_id=1, source_target_pairs={{2,0},{3,1},{0,2},{1,3},{6,4},{7,5},{4,6},{5,7},{10,8},{11,9},{8,1... | collective-permute-start | bytes 835592 | tf_op jit(solution)/shard_map/ppermute | solution.py:514
  105.8 7.0 %collective-permute-start.19 = (bf16[136,1024]{1,0:T(8,128)(2,1)S(1)}, bf16[136,1024]{1,0:T(8,128)(2,1)S(1)}, u32[]{:S(2)}, u32[]{:S(2)}) collective-permute-start(bf16[136,1024]{1,0:T(8,128)(2,1)S(1)} %fusion.4.refs_0_), channel_id=1, source_target_pairs={{8,0},{12,4},{16,8},{20,12},{24,16},{28,20},{0,24},{4,28},{9,1},{1... | collective-permute-start | bytes 835592 | tf_op jit(solution)/shard_map/ppermute | solution.py:474
  105.8 7.0 %collective-permute-start.18 = (bf16[136,1024]{1,0:T(8,128)(2,1)S(1)}, bf16[136,1024]{1,0:T(8,128)(2,1)S(1)}, u32[]{:S(2)}, u32[]{:S(2)}) collective-permute-start(bf16[136,1024]{1,0:T(8,128)(2,1)S(1)} %fusion.4.refs_0_), channel_id=1, source_target_pairs={{4,0},{0,4},{12,8},{8,12},{20,16},{16,20},{28,24},{24,28},{5,1},{1... | collective-permute-start | bytes 835592 | tf_op jit(solution)/shard_map/ppermute | solution.py:482
  106.7 12.2 %collective-permute-start.22 = (bf16[136,1024]{1,0:T(8,128)(2,1)S(1)}, bf16[136,1024]{1,0:T(8,128)(2,1)S(1)}, u32[]{:S(2)}, u32[]{:S(2)}) collective-permute-start(bf16[136,1024]{1,0:T(8,128)(2,1)S(1)} %fusion.4.refs_0_), channel_id=1, source_target_pairs={{24,0},{28,4},{0,8},{4,12},{8,16},{12,20},{16,24},{20,28},{25,1},{... | collective-permute-start | bytes 835592 | tf_op jit(solution)/shard_map/ppermute | solution.py:474
  112.8 6.4 %collective-permute-start.20 = (bf16[136,1024]{1,0:T(8,128)(2,1)S(1)}, bf16[136,1024]{1,0:T(8,128)(2,1)S(1)}, u32[]{:S(2)}, u32[]{:S(2)}) collective-permute-start(bf16[136,1024]{1,0:T(8,128)(2,1)S(1)} %collective-permute-done.19.refs_2_), channel_id=1, source_target_pairs={{4,0},{0,4},{12,8},{8,12},{20,16},{16,20},{28,24},{24,28},{5,1},{1... | collective-permute-start | bytes 835592 | tf_op jit(solution)/shard_map/ppermute | solution.py:482
  112.8 19.6 %collective-permute-start.21 = (bf16[136,1024]{1,0:T(8,128)(2,1)S(1)}, bf16[136,1024]{1,0:T(8,128)(2,1)S(1)}, u32[]{:S(2)}, u32[]{:S(2)}) collective-permute-start(bf16[136,1024]{1,0:T(8,128)(2,1)S(1)} %fusion.4.refs_0_), channel_id=1, source_target_pairs={{16,0},{20,4},{24,8},{28,12},{0,16},{4,20},{8,24},{12,28},{17,1},{... | collective-permute-start | bytes 835592 | tf_op jit(solution)/shard_map/ppermute | solution.py:474
  118.9 13.5 %collective-permute-start.23 = (bf16[136,1024]{1,0:T(8,128)(2,1)S(1)}, bf16[136,1024]{1,0:T(8,128)(2,1)S(1)}, u32[]{:S(2)}, u32[]{:S(2)}) collective-permute-start(bf16[136,1024]{1,0:T(8,128)(2,1)S(1)} %collective-permute-done.22.refs_6_), channel_id=1, source_target_pairs={{4,0},{0,4},{12,8},{8,12},{20,16},{16,20},{28,24},{24,28},{5,1},{1... | collective-permute-start | bytes 835592 | tf_op jit(solution)/shard_map/ppermute | solution.py:482
  132.4 7.7 %collective-permute-start.24 = (bf16[136,1024]{1,0:T(8,128)(2,1)S(1)}, bf16[136,1024]{1,0:T(8,128)(2,1)S(1)}, u32[]{:S(2)}, u32[]{:S(2)}) collective-permute-start(bf16[136,1024]{1,0:T(8,128)(2,1)S(1)} %collective-permute-done.21.refs_4_), channel_id=1, source_target_pairs={{4,0},{0,4},{12,8},{8,12},{20,16},{16,20},{28,24},{24,28},{5,1},{1... | collective-permute-start | bytes 835592 | tf_op jit(solution)/shard_map/ppermute | solution.py:482
  156.9 7.4 %collective-permute-start.26 = (bf16[136,1024]{1,0:T(8,128)(2,1)S(1)}, bf16[136,1024]{1,0:T(8,128)(2,1)S(1)}, u32[]{:S(2)}, u32[]{:S(2)}) collective-permute-start(bf16[136,1024]{1,0:T(8,128)(2,1)S(1)} %get-tuple-element.61), channel_id=1, source_target_pairs={{4,0},{0,4},{12,8},{8,12},{20,16},{16,20},{28,24},{24,28},{5,1},{1... | collective-permute-start | bytes 835592 | tf_op jit(solution)/shard_map/ppermute | solution.py:482
  163.1 6.6 %collective-permute-start.25 = (bf16[136,1024]{1,0:T(8,128)(2,1)S(1)}, bf16[136,1024]{1,0:T(8,128)(2,1)S(1)}, u32[]{:S(2)}, u32[]{:S(2)}) collective-permute-start(bf16[136,1024]{1,0:T(8,128)(2,1)S(1)} %get-tuple-element.56), channel_id=1, source_target_pairs={{4,0},{0,4},{12,8},{8,12},{20,16},{16,20},{28,24},{24,28},{5,1},{1... | collective-permute-start | bytes 835592 | tf_op jit(solution)/shard_map/ppermute | solution.py:482
  164.3 11.3 %collective-permute-start.30 = (bf16[136,1024]{1,0:T(8,128)(2,1)S(1)}, bf16[136,1024]{1,0:T(8,128)(2,1)S(1)}, u32[]{:S(2)}, u32[]{:S(2)}) collective-permute-start(bf16[136,1024]{1,0:T(8,128)(2,1)S(1)} %get-tuple-element.66), channel_id=1, source_target_pairs={{4,0},{0,4},{12,8},{8,12},{20,16},{16,20},{28,24},{24,28},{5,1},{1... | collective-permute-start | bytes 835592 | tf_op jit(solution)/shard_map/ppermute | solution.py:482
  164.7 21.4 %collective-permute-start.27 = (bf16[136,1024]{1,0:T(8,128)(2,1)S(1)}, bf16[136,1024]{1,0:T(8,128)(2,1)S(1)}, u32[]{:S(2)}, u32[]{:S(2)}) collective-permute-start(bf16[136,1024]{1,0:T(8,128)(2,1)S(1)} %add_convert_fusion.4), channel_id=1, source_target_pairs={{16,0},{20,4},{24,8},{28,12},{0,16},{4,20},{8,24},{12,28},{17,1},{... | collective-permute-start | bytes 835592 | tf_op jit(solution)/shard_map/ppermute | solution.py:474
  169.8 17.5 %collective-permute-start.29 = (bf16[136,1024]{1,0:T(8,128)(2,1)S(1)}, bf16[136,1024]{1,0:T(8,128)(2,1)S(1)}, u32[]{:S(2)}, u32[]{:S(2)}) collective-permute-start(bf16[136,1024]{1,0:T(8,128)(2,1)S(1)} %add_convert_fusion.3), channel_id=1, source_target_pairs={{24,0},{28,4},{0,8},{4,12},{8,16},{12,20},{16,24},{20,28},{25,1},{... | collective-permute-start | bytes 835592 | tf_op jit(solution)/shard_map/ppermute | solution.py:474
  175.7 16.3 %collective-permute-start.31 = (bf16[136,1024]{1,0:T(8,128)(2,1)S(1)}, bf16[136,1024]{1,0:T(8,128)(2,1)S(1)}, u32[]{:S(2)}, u32[]{:S(2)}) collective-permute-start(bf16[136,1024]{1,0:T(8,128)(2,1)S(1)} %add_convert_fusion.2), channel_id=1, source_target_pairs={{8,0},{12,4},{16,8},{20,12},{24,16},{28,20},{0,24},{4,28},{9,1},{1... | collective-permute-start | bytes 835592 | tf_op jit(solution)/shard_map/ppermute | solution.py:474
  186.1 7.6 %collective-permute-start.28 = (bf16[136,1024]{1,0:T(8,128)(2,1)S(1)}, bf16[136,1024]{1,0:T(8,128)(2,1)S(1)}, u32[]{:S(2)}, u32[]{:S(2)}) collective-permute-start(bf16[136,1024]{1,0:T(8,128)(2,1)S(1)} %get-tuple-element.62), channel_id=1, source_target_pairs={{4,0},{0,4},{12,8},{8,12},{20,16},{16,20},{28,24},{24,28},{5,1},{1... | collective-permute-start | bytes 835592 | tf_op jit(solution)/shard_map/ppermute | solution.py:482
  194.2 8.1 %collective-permute-start.35 = (bf16[34,1024]{1,0:T(8,128)(2,1)S(1)}, bf16[34,1024]{1,0:T(8,128)(2,1)S(1)}, u32[]{:S(2)}, u32[]{:S(2)}) collective-permute-start(bf16[34,1024]{1,0:T(8,128)(2,1)S(1)} %get-tuple-element.70), channel_id=1, source_target_pairs={{3,0},{11,1},{19,2},{27,3},{7,4},{15,5},{23,6},{31,7},{0,8},{8,9},... | collective-permute-start | bytes 208904 | tf_op jit(solution)/shard_map/ppermute | solution.py:660
  195.9 6.4 %collective-permute-start.34 = (bf16[34,1024]{1,0:T(8,128)(2,1)S(1)}, bf16[34,1024]{1,0:T(8,128)(2,1)S(1)}, u32[]{:S(2)}, u32[]{:S(2)}) collective-permute-start(bf16[34,1024]{1,0:T(8,128)(2,1)S(1)} %get-tuple-element.71), channel_id=1, source_target_pairs={{2,0},{10,1},{18,2},{26,3},{6,4},{14,5},{22,6},{30,7},{3,8},{11,9}... | collective-permute-start | bytes 208904 | tf_op jit(solution)/shard_map/ppermute | solution.py:660
  195.9 6.4 %collective-permute-start.33 = (bf16[34,1024]{1,0:T(8,128)(2,1)S(1)}, bf16[34,1024]{1,0:T(8,128)(2,1)S(1)}, u32[]{:S(2)}, u32[]{:S(2)}) collective-permute-start(bf16[34,1024]{1,0:T(8,128)(2,1)S(1)} %get-tuple-element.72), channel_id=1, source_target_pairs={{1,0},{9,1},{17,2},{25,3},{5,4},{13,5},{21,6},{29,7},{2,8},{10,9},... | collective-permute-start | bytes 208904 | tf_op jit(solution)/shard_map/ppermute | solution.py:660
  196.3 8.4 %collective-permute-start.32 = (bf16[34,1024]{1,0:T(8,128)(2,1)S(1)}, bf16[34,1024]{1,0:T(8,128)(2,1)S(1)}, u32[]{:S(2)}, u32[]{:S(2)}) collective-permute-start(bf16[34,1024]{1,0:T(8,128)(2,1)S(1)} %get-tuple-element.69), channel_id=1, source_target_pairs={{0,0},{8,1},{16,2},{24,3},{4,4},{12,5},{20,6},{28,7},{1,8},{9,9},{... | collective-permute-start | bytes 208904 | tf_op jit(solution)/shard_map/ppermute | solution.py:660
  (27 other events, 154.3 us)
